TPU v7x, 128 devices: a whole 4x4x4 slice. The times are simulated.
128 devices in a mesh: dp: 32 (over z, x, y_hi), heads: 4 (over y_lo, core).
Axes of the slice: x: 4, y: 4 (y_hi: 2, y_lo: 2; y = y_hi * 2 + y_lo), z: 4, core: 2. Of those that a mesh axis runs over, the one named last changes fastest.
Arguments:
- byte_states: bfloat16 [16384, 1280], P('dp'), may hold values from -6 to 6
- patch_states: bfloat16 [4096, 4096], P('dp'), may hold values from -6 to 6
- patch_lengths: int32 [32, 128], P('dp'), may hold values from 1 to 16, 512 in all within a row
- cotangent: bfloat16 [16384, 1280], P('dp'), may hold values from -6 to 6
- attention_gain: float32 [1280], replicated, may hold values from 0.5 to 2
- feedforward_gain: float32 [1280], replicated, may hold values from 0.5 to 1.5
- query_weight: bfloat16 [1280, 1024], P(None, 'heads'), may hold values from -0.15625 to 0.15625
- key_weight: bfloat16 [4096, 1024], P(None, 'heads'), may hold values from -0.09375 to 0.09375
- value_weight: bfloat16 [4096, 1024], P(None, 'heads'), may hold values from -0.09375 to 0.09375
- output_weight: bfloat16 [1024, 1280], P('heads'), may hold values from -0.1875 to 0.1875
- gate_weight: bfloat16 [1280, 3584], P(None, 'heads'), may hold values from -0.15625 to 0.15625
- up_weight: bfloat16 [1280, 3584], P(None, 'heads'), may hold values from -0.15625 to 0.15625
- down_weight: bfloat16 [3584, 1280], P('heads'), may hold values from -0.09375 to 0.09375
- adam_first: float32 [4, 6193152], P('heads', 'dp'), may hold values from -0.6 to 0.6
- adam_second: float32 [4, 6193152], P('heads', 'dp'), may hold values from 0.001 to 0.1
Outputs:
- input_grad: bfloat16 [16384, 1280], P(('dp', 'heads'))
- patch_grad: bfloat16 [4096, 4096], P(('dp', 'heads'))
- new_first: float32 [4, 6193152], P('heads', 'dp')
- new_second: float32 [4, 6193152], P('heads', 'dp')
- adam_step: float32 [4, 6193152], P('heads', 'dp')
Inputs may be any that keep to these rules, and one draw needn't show every extreme that they name: `patch_lengths`: row s holds the lengths in bytes of the 128 patches of sequence s in order; each row sums to 512.
All inputs are finite; a program needn't handle non-finite values.
Results may differ from a plain program's by a relative error of at most 0.039.
Values may be sent and summed in bfloat16 or wider, within the bound.
A program may use at most 128 MiB of HBM per device.

v0:
```python
import jax
import jax.numpy as jnp
from jax import lax
from jax.sharding import PartitionSpec as P

HEAD = 128
BYTES = 512
PATCHES = 128


norm_epsilon = 1e-05
adam_epsilon = 1e-08
beta_first = 0.9
beta_second = 0.95
score_scale = 0.125
bias_first = 1.0 - 0.9**20
bias_second = 1.0 - 0.95**20


def norm_forward(inputs, gain_vec):
    inverse = lax.rsqrt(jnp.mean(inputs * inputs, axis=-1, keepdims=True) + norm_epsilon)
    return inputs * inverse * gain_vec


def norm_backward(inputs, gain_vec, grad_vec):
    inverse = lax.rsqrt(jnp.mean(inputs * inputs, axis=-1, keepdims=True) + norm_epsilon)
    scaled = grad_vec * gain_vec
    inner = jnp.mean(scaled * inputs, axis=-1, keepdims=True)
    return inverse * scaled - inputs * (inverse * inverse * inverse) * inner


def matmul_plain(left, right):
    return jnp.dot(left, right, preferred_element_type=jnp.float32)


def matmul_right_t(left, right):
    return lax.dot_general(
        left, right, (((1,), (1,)), ((), ())), preferred_element_type=jnp.float32
    )


def matmul_left_t(left, right):
    return lax.dot_general(
        left, right, (((0,), (0,)), ((), ())), preferred_element_type=jnp.float32
    )


def spread_piece(grad_local, piece_count):
    return lax.psum_scatter(
        grad_local.reshape(piece_count, -1).astype(jnp.bfloat16),
        "dp",
        scatter_dimension=0,
        tiled=True,
    ).astype(jnp.float32)


def shards(
    byte_states,
    patch_states,
    patch_lengths,
    cotangent,
    attention_gain,
    feedforward_gain,
    query_weight,
    key_weight,
    value_weight,
    output_weight,
    gate_weight,
    up_weight,
    down_weight,
    adam_first,
    adam_second,
):
    row_count = byte_states.shape[0]
    seq_count = patch_lengths.shape[0]
    piece_count = lax.axis_size("dp")
    group_count = lax.axis_size("heads")
    share_rows = row_count // group_count
    group_index = lax.axis_index("heads")
    heads_here = query_weight.shape[1] // HEAD
    byte_float = byte_states.astype(jnp.float32)
    byte_share = lax.dynamic_slice_in_dim(byte_float, group_index * share_rows, share_rows, 0)
    normed_bytes = norm_forward(byte_float, attention_gain).astype(jnp.bfloat16)
    query_full = matmul_plain(normed_bytes, query_weight).reshape(row_count, heads_here, HEAD)
    key_full = matmul_plain(patch_states, key_weight).reshape(-1, heads_here, HEAD)
    value_proj = matmul_plain(patch_states, value_weight).astype(jnp.bfloat16)
    query_seq = (
        norm_forward(query_full, 1.0)
        .astype(jnp.bfloat16)
        .reshape(seq_count, BYTES, heads_here, HEAD)
    )
    key_seq = (
        norm_forward(key_full, 1.0)
        .astype(jnp.bfloat16)
        .reshape(seq_count, PATCHES, heads_here, HEAD)
    )
    value_seq = value_proj.reshape(seq_count, PATCHES, heads_here, HEAD)
    starts = jnp.cumsum(patch_lengths, axis=1) - patch_lengths
    positions = jnp.arange(BYTES, dtype=jnp.int32)
    visible = (starts[:, None, :] <= positions[None, :, None]).astype(jnp.float32)[:, None]
    scores = score_scale * jnp.einsum(
        "sbhd,sphd->shbp", query_seq, key_seq, preferred_element_type=jnp.float32
    )
    weights = jnp.exp(scores) * visible
    probabilities = weights / jnp.sum(weights, axis=-1, keepdims=True)
    prob_half = probabilities.astype(jnp.bfloat16)
    attended = (
        jnp.einsum("shbp,sphd->sbhd", prob_half, value_seq, preferred_element_type=jnp.float32)
        .astype(jnp.bfloat16)
        .reshape(row_count, -1)
    )
    attention_part = matmul_plain(attended, output_weight)
    attention_piece = lax.psum_scatter(
        attention_part.astype(jnp.bfloat16), "heads", scatter_dimension=0, tiled=True
    ).astype(jnp.float32)
    residual_share = byte_share + attention_piece
    normed_share = norm_forward(residual_share, feedforward_gain).astype(jnp.bfloat16)
    normed_hidden = lax.all_gather(normed_share, "heads", axis=0, tiled=True)
    gate = matmul_plain(normed_hidden, gate_weight)
    up_vals = matmul_plain(normed_hidden, up_weight)
    sigmoid = jax.nn.sigmoid(gate)
    activated = gate * sigmoid
    hidden = (activated * up_vals).astype(jnp.bfloat16)
    hidden_grad = matmul_right_t(cotangent, down_weight)
    gate_grad = (hidden_grad * up_vals * (sigmoid * (1.0 + gate * (1.0 - sigmoid)))).astype(
        jnp.bfloat16
    )
    up_grad = (hidden_grad * activated).astype(jnp.bfloat16)
    normed_grad_part = matmul_right_t(gate_grad, gate_weight) + matmul_right_t(up_grad, up_weight)
    grad_gate = matmul_left_t(normed_hidden, gate_grad)
    grad_up = matmul_left_t(normed_hidden, up_grad)
    grad_down = matmul_left_t(hidden, cotangent)
    feedforward_pieces = [
        spread_piece(grad_gate, piece_count),
        spread_piece(grad_up, piece_count),
        spread_piece(grad_down, piece_count),
    ]
    normed_grad_piece = lax.psum_scatter(
        normed_grad_part.astype(jnp.bfloat16), "heads", scatter_dimension=0, tiled=True
    ).astype(jnp.float32)
    cotangent_share = lax.dynamic_slice_in_dim(cotangent, group_index * share_rows, share_rows, 0)
    residual_grad_share = cotangent_share.astype(jnp.float32) + norm_backward(
        residual_share, feedforward_gain, normed_grad_piece
    )
    residual_half = lax.all_gather(
        residual_grad_share.astype(jnp.bfloat16), "heads", axis=0, tiled=True
    )
    attended_grad = matmul_right_t(residual_half, output_weight).astype(jnp.bfloat16)
    attended_seq = attended_grad.reshape(seq_count, BYTES, heads_here, HEAD)
    prob_grad = jnp.einsum(
        "sbhd,sphd->shbp", attended_seq, value_seq, preferred_element_type=jnp.float32
    )
    score_grad = (
        score_scale
        * probabilities
        * (prob_grad - jnp.sum(probabilities * prob_grad, axis=-1, keepdims=True))
    ).astype(jnp.bfloat16)
    query_normed_grad = jnp.einsum(
        "shbp,sphd->sbhd", score_grad, key_seq, preferred_element_type=jnp.float32
    ).reshape(row_count, heads_here, HEAD)
    key_normed_grad = jnp.einsum(
        "shbp,sbhd->sphd", score_grad, query_seq, preferred_element_type=jnp.float32
    ).reshape(-1, heads_here, HEAD)
    value_grad = (
        jnp.einsum("shbp,sbhd->sphd", prob_half, attended_seq, preferred_element_type=jnp.float32)
        .astype(jnp.bfloat16)
        .reshape(-1, heads_here * HEAD)
    )
    query_grad = (
        norm_backward(query_full, 1.0, query_normed_grad)
        .astype(jnp.bfloat16)
        .reshape(row_count, -1)
    )
    key_grad = (
        norm_backward(key_full, 1.0, key_normed_grad)
        .astype(jnp.bfloat16)
        .reshape(-1, heads_here * HEAD)
    )
    bytes_grad_part = matmul_right_t(query_grad, query_weight)
    patch_grad_part = matmul_right_t(key_grad, key_weight) + matmul_right_t(
        value_grad, value_weight
    )
    bytes_grad_piece, patch_grad_piece = (
        lax.psum_scatter(
            bytes_grad_part.astype(jnp.bfloat16), "heads", scatter_dimension=0, tiled=True
        ).astype(jnp.float32),
        lax.psum_scatter(
            patch_grad_part.astype(jnp.bfloat16), "heads", scatter_dimension=0, tiled=True
        ).astype(jnp.float32),
    )
    input_grad = (
        residual_grad_share + norm_backward(byte_share, attention_gain, bytes_grad_piece)
    ).astype(jnp.bfloat16)
    patch_grad = patch_grad_piece.astype(jnp.bfloat16)
    grad_query = matmul_left_t(normed_bytes, query_grad)
    grad_key = matmul_left_t(patch_states, key_grad)
    grad_value = matmul_left_t(patch_states, value_grad)
    grad_output = matmul_left_t(attended, residual_half)
    attention_pieces = [
        spread_piece(grad_item, piece_count)
        for grad_item in (grad_query, grad_key, grad_value, grad_output)
    ]
    summed_grads = jnp.concatenate(attention_pieces + feedforward_pieces, axis=1)
    gradient = summed_grads * float(row_count * piece_count) ** (-0.5)
    new_first = beta_first * adam_first + (1.0 - beta_first) * gradient
    new_second = beta_second * adam_second + (1.0 - beta_second) * gradient * gradient
    adam_step = new_first / bias_first / (jnp.sqrt(new_second / bias_second) + adam_epsilon)
    return (input_grad, patch_grad, new_first, new_second, adam_step)


def solution(mesh):
    placed = (
        P("dp", None),
        P("dp", None),
        P("dp", None),
        P("dp", None),
        P(),
        P(),
        P(None, "heads"),
        P(None, "heads"),
        P(None, "heads"),
        P("heads", None),
        P(None, "heads"),
        P(None, "heads"),
        P("heads", None),
        P("heads", "dp"),
        P("heads", "dp"),
    )
    return jax.shard_map(
        shards,
        mesh=mesh,
        in_specs=placed,
        out_specs=(
            P(("dp", "heads"), None),
            P(("dp", "heads"), None),
            P("heads", "dp"),
            P("heads", "dp"),
            P("heads", "dp"),
        ),
        check_vma=False,
    )
```

profile of v0, /device:TPU:0, one launch (start us, length us, event | category | flops | bytes accessed | tf_op | source)
XLA Modules:
  0.0 783.4 jit_solution(9223321179946133238)
XLA Ops:
  11.5 3.1 multiply_reduce_fusion.6
  17.6 2.1 fusion.7
  20.9 2.2 convolution_convert_fusion.10
  23.1 2.8 convolution_convert_fusion.6
  26.0 3.0 convert_element_type.167
  29.0 21.3 %reduce-scatter.5.cloned.1.call-done = bf16[128,1280]{1,0:T(8,128)(2,1)} async-done(((bf16[512,1280]{1,0:T(8,128)(2,1)}), bf16[128,1280]{1,0:T(8,128)(2,1)}) %reduce-scatter.5.cloned.1.call-update) | async-done | bytes 327696 | tf_op jit(solution)/shard_map/reduce_scatter | solution.py:113
  51.7 2.0 multiply_convert_fusion.5
  53.8 23.7 %all-gather.3.cloned.1.call-done = bf16[512,1280]{1,0:T(8,128)(2,1)} async-done(((bf16[128,1280]{1,0:T(8,128)(2,1)}), bf16[512,1280]{1,0:T(8,128)(2,1)}) %all-gather.3.cloned.1.call-update) | async-done | bytes 1310736 | tf_op jit(solution)/shard_map/all_gather | solution.py:118
  77.5 3.0 fusion.34
  83.2 2.0 multiply_convert_fusion.2
  86.9 2.6 fusion.3
  89.6 22.9 %reduce-scatter.7.cloned.1.call-done = bf16[128,1280]{1,0:T(8,128)(2,1)} async-done(((bf16[512,1280]{1,0:T(8,128)(2,1)}), bf16[128,1280]{1,0:T(8,128)(2,1)}) %reduce-scatter.7.cloned.1.call-update) | async-done | bytes 327696 | tf_op jit(solution)/shard_map/reduce_scatter | solution.py:138
  114.4 2.5 fusion.31
  118.1 3.1 convolution_convert_fusion.4
  121.2 2.5 convert_element_type.207
  123.7 3.1 convolution_convert_fusion.3
  126.8 2.5 convert_element_type.209
  129.3 11.4 %all-gather.5.cloned.1.call-done = bf16[512,1280]{1,0:T(8,128)(2,1)} async-done(((bf16[128,1280]{1,0:T(8,128)(2,1)}), bf16[512,1280]{1,0:T(8,128)(2,1)}) %all-gather.5.cloned.1.call-update) | async-done | bytes 1310736 | tf_op jit(solution)/shard_map/all_gather | solution.py:145
  140.7 2.0 convolution_convert_fusion.9
  146.6 5.3 convolution_convert_fusion.2
  151.9 6.1 convert_element_type.212
  158.5 2.5 convolution_convert_fusion.8
  161.1 2.2 convert_element_type.197
  163.8 2.0 fusion
  165.8 3.3 copy.117
  169.1 2.4 convert_element_type.200
  175.0 3.3 copy.118
  178.3 2.4 convert_element_type.203
  190.2 2.1 add_convert_fusion
  192.3 562.6 %all-reduce.10.cloned.1.call-done = (bf16[32,10240]{1,0:T(8,128)(2,1)}, bf16[32,32768]{1,0:T(8,128)(2,1)}, bf16[32,32768]{1,0:T(8,128)(2,1)}, bf16[32,10240]{1,0...) async-done(((bf16[32,10240]{1,0:T(8,128)(2,1)}, bf16[32,32768]{1,0:T(8,128)(2,1)}, bf16[32,32768]{1,0:T(8,128)(2,1)}, ...) | async-done | bytes 12386320
  765.9 2.1 dynamic-slice_dynamic-update-slice_fusion
  768.0 7.1 add_divide_fusion.1
  (143 shorter events, 47.5 us)
Async XLA Ops:
  7.2 70.3 %copy-start = (bf16[1280,896]{1,0:T(8,128)(2,1)S(1)}, bf16[1280,896]{1,0:T(8,128)(2,1)}, u32[]{:S(2)}) copy-start(bf16[1280,896]{1,0:T(8,128)(2,1)} %param.25) | copy-start | bytes 6881284
  7.2 43.1 %reduce-scatter.5.cloned.1.call-start = ((), (), s32[]{:S(2)}) async-start(), calls=%async_computation.4 | async-start | bytes 1638400 | tf_op jit(solution)/shard_map/reduce_scatter | solution.py:113
  11.4 3.2 copy-start.2
  11.4 3.2 copy-start.5
  11.5 3.2 copy-start.27
  17.6 2.1 copy-start.3
  17.6 2.2 copy-start.11
  17.6 2.2 copy-start.16
  19.7 6.2 copy-start.22
  25.9 25.8 %copy-start.25 = (f32[1280]{0:T(1024)S(1)}, f32[1280]{0:T(1024)}, u32[]{:S(2)}) copy-start(f32[1280]{0:T(1024)} %param.20) | copy-start | bytes 15364
  25.9 51.6 %all-gather.3.cloned.1.call-start = ((), (), s32[]{:S(2)}) async-start(), calls=%async_computation.5 | async-start | bytes 1638400 | tf_op jit(solution)/shard_map/all_gather | solution.py:118
  53.7 58.7 %reduce-scatter.7.cloned.1.call-start = ((), (), s32[]{:S(2)}) async-start(), calls=%async_computation.6 | async-start | bytes 1638400 | tf_op jit(solution)/shard_map/reduce_scatter | solution.py:138
  77.5 3.0 copy-start.31
  77.5 3.0 copy-start.32
  80.5 2.7 copy-start.30
  83.2 2.0 copy-start.36
  86.9 25.6 %copy-start.8 = (bf16[128,1280]{1,0:T(8,128)(2,1)S(1)}, bf16[128,1280]{1,0:T(8,128)(2,1)}, u32[]{:S(2)}) copy-start(bf16[128,1280]{1,0:T(8,128)(2,1)} %reduce-scatter.5.cloned.1.call-done) | copy-start | bytes 983044
  89.5 51.2 %all-gather.5.cloned.1.call-start = ((), (), s32[]{:S(2)}) async-start(), calls=%async_computation.7 | async-start | bytes 1638400 | tf_op jit(solution)/shard_map/all_gather | solution.py:145
  116.9 71.8 %reduce-scatter.9.cloned.1.call-start = ((), (), s32[]{:S(2)}) async-start(), calls=%async_computation.8 | async-start | bytes 1638400 | tf_op jit(solution)/shard_map/reduce_scatter | solution.py:184
  129.3 13.5 %copy-start.23 = (bf16[16,2,8,128]{3,2,1,0:T(8,128)(2,1)S(1)}, bf16[16,2,8,128]{3,2,1,0:T(8,128)(2,1)}, u32[]{:S(2)}) copy-start(bf16[16,2,8,128]{3,2,1,0:T(8,128)(2,1)} %copy-done.22) | copy-start | bytes 196612
  129.3 13.7 %copy-start.19 = (f32[2,512,128]{1,2,0:T(8,128)S(1)}, f32[2,512,128]{1,2,0:T(8,128)}, u32[]{:S(2)}) copy-start(f32[2,512,128]{1,2,0:T(8,128)} %fusion.6) | copy-start | bytes 1572868
  144.6 2.0 copy-start.15
  146.4 608.5 %all-reduce.10.cloned.1.call-start = ((), (), s32[]{:S(2)}) async-start(), calls=%async_computation.10 | async-start | bytes 24772608
  151.9 6.6 copy-start.9
  151.9 6.6 copy-start.26
  151.9 6.6 copy-start.28
  158.5 5.2 copy-start.13
  158.5 5.2 copy-start.20
  178.3 2.4 copy-start.14
  183.7 592.9 %reduce-scatter.11.cloned.1.call-start = ((), (), s32[]{:S(2)}) async-start(), calls=%async_computation.9 | async-start | bytes 1310720 | tf_op jit(solution)/shard_map/reduce_scatter | solution.py:187
  188.7 579.3 %copy-start.17 = (f32[1,193536]{1,0:T(1,128)S(1)}, f32[1,193536]{1,0:T(1,128)}, u32[]{:S(2)}) copy-start(f32[1,193536]{1,0:T(1,128)} %param.29) | copy-start | bytes 2322436
  765.9 10.7 %copy-start.1 = (bf16[1280,896]{1,0:T(8,128)(2,1)S(1)}, bf16[1280,896]{1,0:T(8,128)(2,1)}, u32[]{:S(2)}) copy-start(bf16[1280,896]{1,0:T(8,128)(2,1)} %param.25) | copy-start | bytes 6881284
  (13 other events, 17.8 us)
Sparse Core Ops, SparseCore 0:
  26.0 24.2 reduce-scatter.4
  53.9 23.5 all-gather.2
  89.6 22.7 reduce-scatter.6
  117.1 23.5 all-gather.4
  146.5 22.7 reduce-scatter.8
  183.8 571.0 all-reduce.9
  757.9 18.6 reduce-scatter.10
where the time goes:
time: 786 us; the launch traced here: 783 us
  waiting for transfers between devices  644 us (82%)
  matrix products  51.8 us (7%)
  local copies, waits for them, and re-layouts  45.8 us (6%)
  other arithmetic  26.6 us (3%)
  between operations  14.7 us (2%)
    unnamed x8, waiting for transfers between devices  563 us
    convert_element_type x9, local copies, waits for them, and re-layouts, spread_piece(): grad_local.reshape(piece_count, -1).astype(jnp.bfloat16)  25.6 us
    all_gather x1, waiting for transfers between devices, shards(): normed_hidden = lax.all_gather(normed_share, 'heads', axis=0, tiled=True)  23.7 us
    reduce_scatter x1, waiting for transfers between devices, shards(): lax.psum_scatter(normed_grad_part.astype(jnp.bfloat16), 'heads', scatter_...  22.9 us
    reduce_scatter x1, waiting for transfers between devices, shards(): lax.psum_scatter(attention_part.astype(jnp.bfloat16), 'heads', scatter_di...  21.3 us
    dot_general x7, matrix products, matmul_left_t(): lax.dot_general(left, right, (((0,), (0,)), ((), ())), preferred_element_...  19.9 us
  transfers between devices with their start and end apart: 7, of which 6 were waited for; matrix products, arithmetic and copies ran while one was open for 10% of the time, Pallas kernels for 0%

commit v1 on v0

--- a/solution.py
+++ b/solution.py
@@ -1,6 +1,10 @@
+import functools
+
 import jax
 import jax.numpy as jnp
 from jax import lax
+from jax.experimental import pallas as pl
+from jax.experimental.pallas import tpu as pltpu
 from jax.sharding import PartitionSpec as P
 
 HEAD = 128
@@ -45,13 +49,224 @@
     )
 
 
-def spread_piece(grad_local, piece_count):
-    return lax.psum_scatter(
-        grad_local.reshape(piece_count, -1).astype(jnp.bfloat16),
-        "dp",
-        scatter_dimension=0,
-        tiled=True,
-    ).astype(jnp.float32)
+BF16 = jnp.bfloat16
+F32 = jnp.float32
+MESH_ID = pl.DeviceIdType.MESH
+MIB = 1 << 20
+
+GU1, GU2, DN, KK, VV, QO = range(6)
+PIECES = (
+    (80, 640, True),
+    (80, 256, False),
+    (32, 1280, False),
+    (128, 256, True),
+    (128, 256, False),
+    (80, 256, True),
+)
+FLAT = 1512
+
+
+def place():
+    dp = lax.axis_index("dp")
+    return lax.div(dp, 8), lax.rem(lax.div(dp, 2), 4), lax.rem(dp, 2), lax.axis_index("heads")
+
+
+def device_at(z, x, y, g):
+    return (z * 8 + x * 2 + y, g)
+
+
+def scatter_scratch(items):
+    shapes = []
+    for item in items:
+        rows, cols, _ = PIECES[item]
+        shapes += [
+            pltpu.VMEM((2, 2, 2, rows, cols), BF16),
+            pltpu.VMEM((2, 2, 2, rows, cols), BF16),
+            pltpu.VMEM((2, 4, 2, rows, cols), BF16),
+            pltpu.VMEM((4, 2, rows, cols), BF16),
+            pltpu.VMEM((2, rows, cols), BF16),
+            pltpu.VMEM((2, rows, cols), BF16),
+            pltpu.VMEM((2, 2, rows, cols), BF16),
+            pltpu.VMEM((2, rows, cols), BF16),
+            pltpu.VMEM((rows, cols), BF16),
+            pltpu.SemaphoreType.DMA((13,)),
+            pltpu.SemaphoreType.DMA((13,)),
+        ]
+    return shapes
+
+
+SCATTER_REFS = 11
+
+
+class Scatter:
+    def __init__(self, item, grad, refs):
+        self.grad = grad
+        self.zfirst = PIECES[item][2]
+        (self.near, self.carry, self.got, self.part, self.near2, self.carry2, self.got2, self.pair, self.last,
+         self.send, self.recv) = refs
+        z, x, y, g = place()
+        self.y = y
+        self.f, self.s = (z, x) if self.zfirst else (x, z)
+        self.g = g
+        self.live = {}
+
+    def at(self, f, s):
+        return (f, s) if self.zfirst else (s, f)
+
+    def who(self, f, s, y):
+        z, x = self.at(f, s)
+        return device_at(z, x, y, self.g)
+
+    def copy(self, n, src, dst, dev):
+        c = pltpu.make_async_remote_copy(
+            src_ref=src, dst_ref=dst, send_sem=self.send.at[n], recv_sem=self.recv.at[n],
+            device_id=dev, device_id_type=MESH_ID,
+        )
+        c.start()
+        self.live[n] = c
+
+    def start1(self):
+        for i, d in enumerate((1, 3)):
+            dev = self.who(lax.rem(self.f + d, 4), self.s, self.y)
+            far = lax.rem(self.f + 2, 4)
+            self.copy(i, self.grad.at[self.at(far, pl.ds(2 * i, 2))], self.near.at[i], dev)
+        for i, d in enumerate((1, 3)):
+            nxt = lax.rem(self.f + d, 4)
+            dev = self.who(nxt, self.s, self.y)
+            self.copy(2 + i, self.grad.at[self.at(nxt, pl.ds(2 * (1 - i), 2))], self.got.at[i, pl.ds(2 * (1 - i), 2)], dev)
+
+    def relay1(self):
+        for i, d in enumerate((1, 3)):
+            nxt = lax.rem(self.f + d, 4)
+            dev = self.who(nxt, self.s, self.y)
+            self.live[i].wait_recv()
+
+            @pl.loop(0, 4)
+            def _(k):
+                a, b = lax.div(k, 2), lax.rem(k, 2)
+                own = self.grad[(*self.at(nxt, 2 * i + a), b)].astype(F32)
+                self.carry[i, a, b] = (own + self.near[i, a, b].astype(F32)).astype(BF16)
+
+            self.copy(4 + i, self.carry.at[i], self.got.at[i, pl.ds(2 * i, 2)], dev)
+
+    def start2(self):
+        for n in (2, 3, 4, 5):
+            self.live[n].wait_recv()
+
+        @pl.loop(0, 8)
+        def _(k):
+            a, b = lax.div(k, 2), lax.rem(k, 2)
+            own = self.grad[(*self.at(self.f, a), b)].astype(F32)
+            self.part[a, b] = (own + self.got[0, a, b].astype(F32) + self.got[1, a, b].astype(F32)).astype(BF16)
+
+        for i, d in enumerate((1, 3)):
+            dev = self.who(self.f, lax.rem(self.s + d, 4), self.y)
+            self.copy(6 + i, self.part.at[lax.rem(self.s + 2, 4), i], self.near2.at[i], dev)
+        for i, d in enumerate((1, 3)):
+            nxt = lax.rem(self.s + d, 4)
+            dev = self.who(self.f, nxt, self.y)
+            self.copy(8 + i, self.part.at[nxt, 1 - i], self.got2.at[i, 1 - i], dev)
+
+    def relay2(self):
+        for i, d in enumerate((1, 3)):
+            nxt = lax.rem(self.s + d, 4)
+            dev = self.who(self.f, nxt, self.y)
+            self.live[6 + i].wait_recv()
+            self.carry2[i] = (self.part[nxt, i].astype(F32) + self.near2[i].astype(F32)).astype(BF16)
+            self.copy(10 + i, self.carry2.at[i], self.got2.at[i, i], dev)
+
+    def start3(self):
+        for n in (8, 9, 10, 11):
+            self.live[n].wait_recv()
+        for b in range(2):
+            own = self.part[self.s, b].astype(F32)
+            self.pair[b] = (own + self.got2[0, b].astype(F32) + self.got2[1, b].astype(F32)).astype(BF16)
+        other = 1 - self.y
+        self.copy(12, self.pair.at[other], self.last, self.who(self.f, self.s, other))
+
+    def finish(self):
+        self.live[12].wait_recv()
+        return self.pair[self.y].astype(F32) + self.last[...].astype(F32)
+
+    def drain(self):
+        for n in range(13):
+            self.live[n].wait_send()
+
+
+def spread_rows(flat, base, per_row, first, block):
+    rows, cols = block.shape
+    for c in range(cols // 128):
+        flat[pl.ds(base + first + c, rows, per_row), :] = block[:, c * 128 : (c + 1) * 128]
+
+
+def place_piece(item, total, flat):
+    if item == QO:
+        spread_rows(flat, 0, 2, 0, total[0:40])
+        for j in range(5):
+            spread_rows(flat, 592, 10, 2 * j, total[40 + 8 * j : 48 + 8 * j])
+    elif item == KK:
+        spread_rows(flat, 80, 2, 0, total)
+    elif item == VV:
+        spread_rows(flat, 336, 2, 0, total)
+    elif item == DN:
+        spread_rows(flat, 1232, 10, 0, total[0:28])
+    else:
+        first = 0 if item == GU1 else 5
+        spread_rows(flat, 672, 7, first, total[0:40])
+        spread_rows(flat, 952, 7, first, total[40:80])
+
+
+def greet(devices):
+    barrier = pltpu.get_barrier_semaphore()
+    for dev in devices:
+        pl.semaphore_signal(barrier, inc=1, device_id=dev, device_id_type=MESH_ID)
+    pl.semaphore_wait(barrier, len(devices))
+
+
+def dp_partners():
+    z, x, y, g = place()
+    return [
+        device_at(lax.rem(z + 1, 4), x, y, g),
+        device_at(lax.rem(z + 3, 4), x, y, g),
+        device_at(z, lax.rem(x + 1, 4), y, g),
+        device_at(z, lax.rem(x + 3, 4), y, g),
+        device_at(z, x, 1 - y, g),
+    ]
+
+
+def scatter_kernel(*refs):
+    count = len(PIECES)
+    grads, flat, rest = refs[:count], refs[count], refs[count + 1 :]
+    jobs = [Scatter(i, grads[i], rest[SCATTER_REFS * i : SCATTER_REFS * (i + 1)]) for i in range(count)]
+    greet(dp_partners())
+    for job in jobs:
+        job.start1()
+    for job in jobs:
+        job.relay1()
+    for i in range(count + 2):
+        if i < count:
+            jobs[i].start2()
+        if 0 <= i - 1 < count:
+            jobs[i - 1].relay2()
+        if 0 <= i - 2 < count:
+            jobs[i - 2].start3()
+    for i in range(count):
+        place_piece(i, jobs[i].finish(), flat)
+    for job in jobs:
+        job.drain()
+
+
+def scatter_grads(grads):
+    return pl.pallas_call(
+        scatter_kernel,
+        out_shape=jax.ShapeDtypeStruct((FLAT, 128), F32),
+        in_specs=[pl.BlockSpec(memory_space=pltpu.VMEM)] * len(PIECES),
+        out_specs=pl.BlockSpec(memory_space=pltpu.VMEM),
+        scratch_shapes=scatter_scratch(range(len(PIECES))),
+        compiler_params=pltpu.CompilerParams(
+            collective_id=0, has_side_effects=True, vmem_limit_bytes=56 * MIB
+        ),
+    )(*grads)
 
 
 def shards(
@@ -95,7 +310,8 @@
         .reshape(seq_count, PATCHES, heads_here, HEAD)
     )
     value_seq = value_proj.reshape(seq_count, PATCHES, heads_here, HEAD)
-    starts = jnp.cumsum(patch_lengths, axis=1) - patch_lengths
+    before = jnp.arange(PATCHES)[None, :] < jnp.arange(PATCHES)[:, None]
+    starts = jnp.sum(jnp.where(before[None], patch_lengths[:, None, :], 0), axis=-1)
     positions = jnp.arange(BYTES, dtype=jnp.int32)
     visible = (starts[:, None, :] <= positions[None, :, None]).astype(jnp.float32)[:, None]
     scores = score_scale * jnp.einsum(
@@ -130,11 +346,6 @@
     grad_gate = matmul_left_t(normed_hidden, gate_grad)
     grad_up = matmul_left_t(normed_hidden, up_grad)
     grad_down = matmul_left_t(hidden, cotangent)
-    feedforward_pieces = [
-        spread_piece(grad_gate, piece_count),
-        spread_piece(grad_up, piece_count),
-        spread_piece(grad_down, piece_count),
-    ]
     normed_grad_piece = lax.psum_scatter(
         normed_grad_part.astype(jnp.bfloat16), "heads", scatter_dimension=0, tiled=True
     ).astype(jnp.float32)
@@ -196,16 +407,31 @@
     grad_key = matmul_left_t(patch_states, key_grad)
     grad_value = matmul_left_t(patch_states, value_grad)
     grad_output = matmul_left_t(attended, residual_half)
-    attention_pieces = [
-        spread_piece(grad_item, piece_count)
-        for grad_item in (grad_query, grad_key, grad_value, grad_output)
-    ]
-    summed_grads = jnp.concatenate(attention_pieces + feedforward_pieces, axis=1)
-    gradient = summed_grads * float(row_count * piece_count) ** (-0.5)
+    gate_up = jnp.concatenate([grad_gate.reshape(32, 40, -1), grad_up.reshape(32, 40, -1)], axis=1).astype(BF16)
+    down = jnp.pad(grad_down.reshape(32, 28, -1).astype(BF16), ((0, 0), (0, 4), (0, 0)))
+    out_blocks = jnp.swapaxes(grad_output.reshape(32, 8, 5, 256), 1, 2).reshape(32, 40, 256)
+    query_out = jnp.concatenate([grad_query.reshape(32, 40, 256), out_blocks], axis=1).astype(BF16)
+    grads = [None] * 6
+    grads[GU1] = gate_up[:, :, :640]
+    grads[GU2] = gate_up[:, :, 640:]
+    grads[DN] = down
+    grads[KK] = grad_key.astype(BF16)
+    grads[VV] = grad_value.astype(BF16)
+    grads[QO] = query_out
+    summed = scatter_grads([m.reshape(4, 4, 2, r, c) for m, (r, c, _) in zip(grads, PIECES)])
+    gradient = summed * float(row_count * piece_count) ** (-0.5)
+    adam_first = adam_first.reshape(FLAT, 128)
+    adam_second = adam_second.reshape(FLAT, 128)
     new_first = beta_first * adam_first + (1.0 - beta_first) * gradient
     new_second = beta_second * adam_second + (1.0 - beta_second) * gradient * gradient
     adam_step = new_first / bias_first / (jnp.sqrt(new_second / bias_second) + adam_epsilon)
-    return (input_grad, patch_grad, new_first, new_second, adam_step)
+    return (
+        input_grad,
+        patch_grad,
+        new_first.reshape(1, -1),
+        new_second.reshape(1, -1),
+        adam_step.reshape(1, -1),
+    )
 
 
 def solution(mesh):

time: 786 us -> 282 us (0.36)
  waiting for transfers between devices: 644 us -> 73.3 us
  Pallas kernels: 0 us -> 87.4 us
  local copies, waits for them, and re-layouts: 45.8 us -> 24.5 us
  other arithmetic: 26.6 us -> 35.3 us
    unnamed x8 -> x6, waiting for transfers between devices: 563 us -> 0.1 us
    pallas_call x0 -> x1, Pallas kernels: none -> 87.4 us  [scatter_grads(): pl.pallas_call(scatter_kernel, out_shape=jax.ShapeDtypeStruct((FLAT, 128)...]
    convert_element_type x9 -> x3, local copies, waits for them, and re-layouts: 25.6 us -> 9.2 us  [the longest x1 4.12 us: shards(): grad_down.reshape(32, 28, -1).astype(BF16)]
    unnamed x83 -> x98, local copies, waits for them, and re-layouts: 14.8 us -> 3.41 us
  transfers between devices with their start and end apart: 7 -> 6, of which waited for: 6 -> 4; matrix products, arithmetic and copies ran while one was open for 10% -> 21% of each run, Pallas kernels for 0% -> 31%
where the time goes in v1:
time: 282 us
  Pallas kernels  87.4 us (31%)
  waiting for transfers between devices  73.3 us (26%)
  matrix products  45.7 us (16%)
  other arithmetic  35.3 us (13%)
  local copies, waits for them, and re-layouts  24.5 us (9%)
  between operations  14.7 us (5%)
    pallas_call x1, Pallas kernels, scatter_grads(): pl.pallas_call(scatter_kernel, out_shape=jax.ShapeDtypeStruct((FLAT, 128)...  87.4 us
    all_gather x1, waiting for transfers between devices, shards(): normed_hidden = lax.all_gather(normed_share, 'heads', axis=0, tiled=True)  23.7 us
    reduce_scatter x1, waiting for transfers between devices, shards(): lax.psum_scatter(attention_part.astype(jnp.bfloat16), 'heads', scatter_di...  21.3 us
    reduce_scatter x1, waiting for transfers between devices, shards(): lax.psum_scatter(normed_grad_part.astype(jnp.bfloat16), 'heads', scatter_...  21.3 us
    dot_general x7, matrix products, matmul_left_t(): lax.dot_general(left, right, (((0,), (0,)), ((), ())), preferred_element_...  13.7 us
    dot_general x6, matrix products, matmul_plain(): return jnp.dot(left, right, preferred_element_type=jnp.float32)  13.6 us
    dot_general x7, matrix products, matmul_right_t(): lax.dot_general(left, right, (((1,), (1,)), ((), ())), preferred_element_...  12.6 us
    all_gather x1, waiting for transfers between devices, shards(): lax.all_gather(residual_grad_share.astype(jnp.bfloat16), 'heads', axis=0,...  6.9 us
  transfers between devices with their start and end apart: 6, of which 4 were waited for; matrix products, arithmetic and copies ran while one was open for 21% of the time, Pallas kernels for 31%

profile of v1, /device:TPU:0, one launch (start us, length us, event | category | flops | bytes accessed | tf_op | source)
XLA Modules:
  0.0 281.7 jit_solution(13317057096925276597)
XLA Ops:
  10.6 3.1 %multiply_reduce_fusion.6 = (f32[512,2]{0,1:T(2,128)S(1)}, f32[512,256]{0,1:T(8,128)}) fusion(bf16[1280,256]{1,0:T(8,128)(2,1)} %param.21, f32[1280]{0:T(1024)} %param.19, f32[512]{0:T(512)S(1)} %add_rsqrt_fusion.1, bf16[512,1280]{1,0:T(8,128)(2,1)} %param.15), kind=kOutput, calls=%fused_computation.58 | convolution fusion | flops 338426880 | bytes 2501632 | tf_op jit(solution)/shard_map/dot_general | solution.py:37
  17.9 2.0 fusion.8
  21.0 2.3 convolution_convert_fusion.10
  23.3 2.8 convolution_convert_fusion.6
  26.2 3.0 %convert_element_type.135 = f32[512,1280]{1,0:T(8,128)} convert(bf16[512,1280]{1,0:T(8,128)(2,1)} %param.15) | non-fusion elementwise | flops 655360 | bytes 3932160 | tf_op jit(solution)/shard_map/convert_element_type | solution.py:296
  29.2 21.3 %reduce-scatter.5.cloned.1.call-done = bf16[128,1280]{1,0:T(8,128)(2,1)} async-done(((bf16[512,1280]{1,0:T(8,128)(2,1)}), bf16[128,1280]{1,0:T(8,128)(2,1)}) %reduce-scatter.5.cloned.1.call-update) | async-done | bytes 327696 | tf_op jit(solution)/shard_map/reduce_scatter | solution.py:329
  51.9 2.0 multiply_convert_fusion.5
  54.0 23.7 %all-gather.3.cloned.1.call-done = bf16[512,1280]{1,0:T(8,128)(2,1)} async-done(((bf16[128,1280]{1,0:T(8,128)(2,1)}), bf16[512,1280]{1,0:T(8,128)(2,1)}) %all-gather.3.cloned.1.call-update) | async-done | bytes 1310736 | tf_op jit(solution)/shard_map/all_gather | solution.py:334
  77.7 3.0 %fusion.37 = f32[512,896]{1,0:T(8,128)S(1)} fusion(bf16[512,1280]{1,0:T(8,128)(2,1)} %all-gather.3.cloned.1.call-done, bf16[1280,896]{1,0:T(8,128)(2,1)S(1)} %copy-done), kind=kOutput, calls=%fused_computation.106 | convolution fusion | flops 1174405120 | bytes 5439488 | tf_op jit(solution)/shard_map/dot_general | solution.py:37
  83.5 2.0 multiply_convert_fusion.2
  87.1 2.6 fusion.4
  91.4 21.3 %reduce-scatter.7.cloned.1.call-done = bf16[128,1280]{1,0:T(8,128)(2,1)} async-done(((bf16[512,1280]{1,0:T(8,128)(2,1)}), bf16[128,1280]{1,0:T(8,128)(2,1)}) %reduce-scatter.7.cloned.1.call-update) | async-done | bytes 327696 | tf_op jit(solution)/shard_map/reduce_scatter | solution.py:349
  112.7 1.9 multiply_reduce_fusion.2
  114.6 2.6 fusion.34
  117.5 2.6 broadcast_multiply_fusion.1
  122.4 2.4 copy.155
  124.8 3.3 %convolution_convert_fusion.4 = bf16[1280,896]{1,0:T(8,128)(2,1)S(1)} fusion(bf16[512,1280]{1,0:T(8,128)(2,1)} %all-gather.3.cloned.1.call-done, bf16[512,896]{1,0:T(8,128)(2,1)} %copy-done.48), kind=kOutput, calls=%fused_computation.10 | convolution fusion | flops 1175552000 | bytes 4521984 | tf_op jit(solution)/shard_map/dot_general | solution.py:47
  128.1 3.1 %convolution_convert_fusion.3 = bf16[1280,896]{1,0:T(8,128)(2,1)} fusion(bf16[512,1280]{1,0:T(8,128)(2,1)S(1)} %copy-done.41, bf16[512,896]{1,0:T(8,128)(2,1)S(1)} %copy-done.43), kind=kOutput, calls=%fused_computation.9 | convolution fusion | flops 1175552000 | bytes 4521984 | tf_op jit(solution)/shard_map/dot_general | solution.py:47
  131.2 2.9 %convolution_convert_fusion.2 = bf16[896,1280]{1,0:T(8,128)(2,1)} fusion(bf16[512,1280]{1,0:T(8,128)(2,1)S(1)} %copy-done.29, f32[512,896]{1,0:T(8,128)S(1)} %copy-done.47, f32[512,896]{1,0:T(8,128)S(1)} %copy-done.45), kind=kOutput, calls=%fused_computation.8 | convolution fusion | flops 1178304512 | bytes 7274496 | tf_op jit(solution)/shard_map/dot_general | solution.py:47
  134.1 6.9 %all-gather.5.cloned.1.call-done = bf16[512,1280]{1,0:T(8,128)(2,1)} async-done(((bf16[128,1280]{1,0:T(8,128)(2,1)}), bf16[512,1280]{1,0:T(8,128)(2,1)}) %all-gather.5.cloned.1.call-update) | async-done | bytes 1310736 | tf_op jit(solution)/shard_map/all_gather | solution.py:356
  141.0 2.1 convolution_convert_fusion.9
  145.8 1.7 convolution_convert_fusion.5
  147.8 3.0 %fusion.3 = bf16[32,80,640]{2,1,0:T(8,128)(2,1)} fusion(bf16[32,40,896]{2,1,0:T(8,128)(2,1)S(1)} %bitcast.156, bf16[32,40,896]{2,1,0:T(8,128)(2,1)} %bitcast.158), kind=kLoop, calls=%fused_computation.12 | loop fusion | flops 6553600 | bytes 7864320 | tf_op jit(solution)/shard_map/concatenate | solution.py:410
  150.7 4.1 %convert_element_type.166 = bf16[32,28,1280]{2,1,0:T(8,128)(2,1)} reshape(bf16[896,1280]{1,0:T(8,128)(2,1)} %convolution_convert_fusion.2) | data formatting | bytes 4587520 | tf_op jit(solution)/shard_map/convert_element_type | solution.py:411
  154.9 3.7 %pad.4 = bf16[32,32,1280]{2,1,0:T(8,128)(2,1)} pad(bf16[32,28,1280]{2,1,0:T(8,128)(2,1)} %convert_element_type.166, bf16[]{:T(256)} %constant.50.clone.1), padding=0_0x0_4x0_0 | pad | bytes 4915202 | tf_op jit(solution)/shard_map/jit(_pad)/pad | solution.py:411
  163.0 2.6 copy.153
  167.9 2.5 copy.154
  170.4 2.6 copy.157
  174.6 1.8 fusion.2
  180.7 87.4 %shard_map.182 = f32[1512,128]{1,0:T(8,128)} custom-call(bf16[4,4,2,80,640]{4,3,2,1,0:T(8,128)(2,1)} %bitcast.154, bf16[4,4,2,80,256]{4,3,2,1,0:T(8,128)(2,1)} %bitcast.165, bf16[4,4,2,32,1280]{4,3,2,1,0:T(8,128)(2,1)} %bitcast.155, bf16[4,4,2,128,256]{4,3,2,1,0:T(8,128)(2,1)} %bitcast.160, bf16[4,4,2,128,256]{4,3,2,1,0:T(8,128)(2,1)} %bitcast.161, ...), custom_call_target="tpu_custom_call" | custom-call | tf_op jit(solution)/shard_map/pallas_call | solution.py:260
  268.2 2.9 %add_divide_fusion.1 = (f32[1512,128]{1,0:T(8,128)}, f32[1512,128]{1,0:T(8,128)}, f32[1512,128]{1,0:T(8,128)}) fusion(f32[1512,128]{1,0:T(8,128)S(1)} %bitcast.167, f32[1512,128]{1,0:T(8,128)} %shard_map.182, f32[1512,128]{1,0:T(8,128)S(1)} %bitcast.168), kind=kLoop, calls=%fused_computation.35 | loop fusion | flops 1935360 | bytes 4644864 | tf_op jit(solution)/shard_map/div | solution.py:427
  272.5 2.3 add_convert_fusion
  (157 shorter events, 35.4 us)
Async XLA Ops:
  7.2 70.6 %copy-start = (bf16[1280,896]{1,0:T(8,128)(2,1)S(1)}, bf16[1280,896]{1,0:T(8,128)(2,1)}, u32[]{:S(2)}) copy-start(bf16[1280,896]{1,0:T(8,128)(2,1)} %param.25) | copy-start | bytes 6881284
  7.2 43.3 %reduce-scatter.5.cloned.1.call-start = ((), (), s32[]{:S(2)}) async-start(), calls=%async_computation.4 | async-start | bytes 1638400 | tf_op jit(solution)/shard_map/reduce_scatter | solution.py:329
  10.6 3.8 %copy-start.2 = (bf16[128,4096]{1,0:T(8,128)(2,1)S(1)}, bf16[128,4096]{1,0:T(8,128)(2,1)}, u32[]{:S(2)}) copy-start(bf16[128,4096]{1,0:T(8,128)(2,1)} %param.16) | copy-start | bytes 3145732
  10.6 3.8 %copy-start.8 = (bf16[4096,256]{1,0:T(8,128)(2,1)S(1)}, bf16[4096,256]{1,0:T(8,128)(2,1)}, u32[]{:S(2)}) copy-start(bf16[4096,256]{1,0:T(8,128)(2,1)} %param.22) | copy-start | bytes 6291460
  10.6 3.8 %copy-start.33 = (f32[512]{0:T(512)}, f32[512]{0:T(512)S(1)}, u32[]{:S(2)}) copy-start(f32[512]{0:T(512)S(1)} %add_rsqrt_fusion.1) | copy-start | bytes 6148
  17.3 2.7 copy-start.21
  19.9 6.2 %copy-start.26 = (bf16[16,2,8,128]{3,2,1,0:T(8,128)(2,1)}, bf16[16,2,8,128]{3,2,1,0:T(8,128)(2,1)S(1)}, u32[]{:S(2)}) copy-start(bf16[16,2,8,128]{3,2,1,0:T(8,128)(2,1)S(1)} %fusion.8) | copy-start | bytes 196612
  26.1 25.8 %copy-start.30 = (f32[1280]{0:T(1024)S(1)}, f32[1280]{0:T(1024)}, u32[]{:S(2)}) copy-start(f32[1280]{0:T(1024)} %param.20) | copy-start | bytes 15364
  26.1 51.6 %all-gather.3.cloned.1.call-start = ((), (), s32[]{:S(2)}) async-start(), calls=%async_computation.5 | async-start | bytes 1638400 | tf_op jit(solution)/shard_map/all_gather | solution.py:334
  54.0 58.7 %reduce-scatter.7.cloned.1.call-start = ((), (), s32[]{:S(2)}) async-start(), calls=%async_computation.6 | async-start | bytes 1638400 | tf_op jit(solution)/shard_map/reduce_scatter | solution.py:349
  77.7 3.0 %copy-start.39 = (bf16[1280,896]{1,0:T(8,128)(2,1)S(1)}, bf16[1280,896]{1,0:T(8,128)(2,1)}, u32[]{:S(2)}) copy-start(bf16[1280,896]{1,0:T(8,128)(2,1)} %param.26) | copy-start | bytes 6881284
  77.7 3.0 %copy-start.40 = (bf16[512,1280]{1,0:T(8,128)(2,1)S(1)}, bf16[512,1280]{1,0:T(8,128)(2,1)}, u32[]{:S(2)}) copy-start(bf16[512,1280]{1,0:T(8,128)(2,1)} %all-gather.3.cloned.1.call-done) | copy-start | bytes 3932164
  80.8 2.7 copy-start.38
  87.1 2.7 copy-start.22
  89.7 22.9 %copy-start.13 = (bf16[128,1280]{1,0:T(8,128)(2,1)S(1)}, bf16[128,1280]{1,0:T(8,128)(2,1)}, u32[]{:S(2)}) copy-start(bf16[128,1280]{1,0:T(8,128)(2,1)} %reduce-scatter.5.cloned.1.call-done) | copy-start | bytes 983044
  89.8 51.2 %all-gather.5.cloned.1.call-start = ((), (), s32[]{:S(2)}) async-start(), calls=%async_computation.7 | async-start | bytes 1638400 | tf_op jit(solution)/shard_map/all_gather | solution.py:356
  114.6 5.4 %copy-start.35 = (f32[128,2]{0,1:T(2,128)S(1)}, f32[128,2]{0,1:T(2,128)}, u32[]{:S(2)}) copy-start(f32[128,2]{0,1:T(2,128)} %get-tuple-element.16) | copy-start | bytes 3076
  114.6 6.3 %copy-start.3 = (bf16[512,1280]{1,0:T(8,128)(2,1)S(1)}, bf16[512,1280]{1,0:T(8,128)(2,1)}, u32[]{:S(2)}) copy-start(bf16[512,1280]{1,0:T(8,128)(2,1)} %param.15) | copy-start | bytes 3932164
  114.6 6.3 %copy-start.31 = (f32[1280]{0:T(1024)S(1)}, f32[1280]{0:T(1024)}, u32[]{:S(2)}) copy-start(f32[1280]{0:T(1024)} %param.19) | copy-start | bytes 15364
  114.6 6.3 %copy-start.34 = (f32[512]{0:T(512)S(1)}, f32[512]{0:T(512)}, u32[]{:S(2)}) copy-start(f32[512]{0:T(512)} %copy-done.33) | copy-start | bytes 6148
  117.3 153.8 %reduce-scatter.9.cloned.1.call-start = ((), (), s32[]{:S(2)}) async-start(), calls=%async_computation.8 | async-start | bytes 1638400 | tf_op jit(solution)/shard_map/reduce_scatter | solution.py:395
  124.8 3.3 %copy-start.41 = (bf16[512,1280]{1,0:T(8,128)(2,1)S(1)}, bf16[512,1280]{1,0:T(8,128)(2,1)}, u32[]{:S(2)}) copy-start(bf16[512,1280]{1,0:T(8,128)(2,1)} %all-gather.3.cloned.1.call-done) | copy-start | bytes 3932164
  124.8 3.3 %copy-start.43 = (bf16[512,896]{1,0:T(8,128)(2,1)S(1)}, bf16[512,896]{1,0:T(8,128)(2,1)}, u32[]{:S(2)}) copy-start(bf16[512,896]{1,0:T(8,128)(2,1)} %copy-done.42) | copy-start | bytes 2752516
  128.1 3.1 %copy-start.29 = (bf16[512,1280]{1,0:T(8,128)(2,1)S(1)}, bf16[512,1280]{1,0:T(8,128)(2,1)}, u32[]{:S(2)}) copy-start(bf16[512,1280]{1,0:T(8,128)(2,1)} %param.18) | copy-start | bytes 3932164
  128.1 3.1 %copy-start.45 = (f32[512,896]{1,0:T(8,128)S(1)}, f32[512,896]{1,0:T(8,128)}, u32[]{:S(2)}) copy-start(f32[512,896]{1,0:T(8,128)} %copy-done.44) | copy-start | bytes 5505028
  128.1 3.1 %copy-start.47 = (f32[512,896]{1,0:T(8,128)S(1)}, f32[512,896]{1,0:T(8,128)}, u32[]{:S(2)}) copy-start(f32[512,896]{1,0:T(8,128)} %copy-done.46) | copy-start | bytes 5505028
  147.5 127.3 %reduce-scatter.11.cloned.1.call-start = ((), (), s32[]{:S(2)}) async-start(), calls=%async_computation.9 | async-start | bytes 1310720 | tf_op jit(solution)/shard_map/reduce_scatter | solution.py:398
  154.9 3.7 %copy-start.4 = (bf16[1280,896]{1,0:T(8,128)(2,1)S(1)}, bf16[1280,896]{1,0:T(8,128)(2,1)}, u32[]{:S(2)}) copy-start(bf16[1280,896]{1,0:T(8,128)(2,1)} %convolution_convert_fusion.3) | copy-start | bytes 6881284
  180.7 87.4 %copy-start.14 = (f32[1,193536]{1,0:T(1,128)S(1)}, f32[1,193536]{1,0:T(1,128)}, u32[]{:S(2)}) copy-start(f32[1,193536]{1,0:T(1,128)} %broadcast_multiply_fusion) | copy-start | bytes 2322436
  180.7 87.4 %copy-start.15 = (f32[1,193536]{1,0:T(1,128)S(1)}, f32[1,193536]{1,0:T(1,128)}, u32[]{:S(2)}) copy-start(f32[1,193536]{1,0:T(1,128)} %broadcast_multiply_fusion.1) | copy-start | bytes 2322436
  268.2 4.3 %copy-start.37 = (f32[128]{0:T(128)S(1)}, f32[128]{0:T(128)}, u32[]{:S(2)}) copy-start(f32[128]{0:T(128)} %get-tuple-element.19) | copy-start | bytes 1540
  268.2 6.6 %copy-start.1 = (bf16[1280,896]{1,0:T(8,128)(2,1)S(1)}, bf16[1280,896]{1,0:T(8,128)(2,1)}, u32[]{:S(2)}) copy-start(bf16[1280,896]{1,0:T(8,128)(2,1)} %param.25) | copy-start | bytes 6881284
  (23 other events, 38.9 us)
Sparse Core Ops, SparseCore 0:
  26.2 24.2 reduce-scatter.4
  54.1 23.5 all-gather.2
  89.9 22.7 reduce-scatter.6
  117.4 23.5 all-gather.4
  147.6 22.7 reduce-scatter.8
  176.5 20.9 reduce-scatter.10

commit v2 on v1

v2 whole, which is shorter than its diff:
```python
import jax
import jax.numpy as jnp
from jax import lax
from jax.experimental import pallas as pl
from jax.experimental.pallas import tpu as pltpu
from jax.sharding import PartitionSpec as P

HEAD = 128

norm_epsilon = 1e-05
adam_epsilon = 1e-08
beta_first = 0.9
beta_second = 0.95
score_scale = 0.125
bias_first = 1.0 - 0.9**20
bias_second = 1.0 - 0.95**20

BF16 = jnp.bfloat16
F32 = jnp.float32
MESH_ID = pl.DeviceIdType.MESH
MIB = 1 << 20

D = 1280
DG = 4096
UNITS = 896
UNIT_TILES = ((0, 256), (256, 512), (512, 768), (768, 896))
WIDE_TILES = tuple((n, n + 256) for n in range(0, D, 256))
FLAT = 1512

GU1, GU2, DN, KK, VV, QO = range(6)
PIECES = (
    (80, 640, True),
    (80, 256, False),
    (32, 1280, False),
    (128, 256, True),
    (128, 256, False),
    (160, 128, True),
)


def nn(left, right):
    return lax.dot_general(left, right, (((1,), (0,)), ((), ())), preferred_element_type=F32)


def nt(left, right):
    return lax.dot_general(left, right, (((1,), (1,)), ((), ())), preferred_element_type=F32)


def tn(left, right):
    return lax.dot_general(left, right, (((0,), (0,)), ((), ())), preferred_element_type=F32)


def inverse_rms(x):
    return lax.rsqrt(jnp.mean(x * x, axis=-1, keepdims=True) + norm_epsilon)


def norm_backward(x, inverse, scaled):
    inner = jnp.mean(scaled * x, axis=-1, keepdims=True)
    return inverse * scaled - x * (inverse * inverse * inverse) * inner


def place():
    dp = lax.axis_index("dp")
    return lax.div(dp, 8), lax.rem(lax.div(dp, 2), 4), lax.rem(dp, 2), lax.axis_index("heads")


def device_at(z, x, y, g):
    return (z * 8 + x * 2 + y, g)


def remote(src, dst, send, recv, dev):
    return pltpu.make_async_remote_copy(
        src_ref=src, dst_ref=dst, send_sem=send, recv_sem=recv, device_id=dev, device_id_type=MESH_ID
    )


def scatter_scratch(item):
    rows, cols, _ = PIECES[item]
    return [
        pltpu.VMEM((4, 4, 2, rows, cols), BF16),
        pltpu.VMEM((2, 2, 2, rows, cols), BF16),
        pltpu.VMEM((2, 4, 2, rows, cols), BF16),
        pltpu.VMEM((2, rows, cols), BF16),
        pltpu.VMEM((2, 2, rows, cols), BF16),
        pltpu.VMEM((rows, cols), BF16),
        pltpu.SemaphoreType.DMA((13,)),
        pltpu.SemaphoreType.DMA((13,)),
    ]


class Scatter:
    def __init__(self, item, refs):
        self.zfirst = PIECES[item][2]
        self.grad, self.near, self.got, self.near2, self.got2, self.last, self.send, self.recv = refs
        z, x, self.y, self.g = place()
        self.f, self.s = (z, x) if self.zfirst else (x, z)
        self.live = {}

    def at(self, f, s):
        return (f, s) if self.zfirst else (s, f)

    def mine(self, s, y):
        return (*self.at(self.f, s), y)

    def who(self, f, s, y):
        z, x = self.at(f, s)
        return device_at(z, x, y, self.g)

    def copy(self, n, src, dst, dev):
        c = remote(src, dst, self.send.at[n], self.recv.at[n], dev)
        c.start()
        self.live[n] = c

    def start1(self):
        far = lax.rem(self.f + 2, 4)
        for i, d in enumerate((1, 3)):
            dev = self.who(lax.rem(self.f + d, 4), self.s, self.y)
            self.copy(i, self.grad.at[self.at(far, pl.ds(2 * i, 2))], self.near.at[i], dev)
        for i, d in enumerate((1, 3)):
            nxt = lax.rem(self.f + d, 4)
            dev = self.who(nxt, self.s, self.y)
            rest = pl.ds(2 * (1 - i), 2)
            self.copy(2 + i, self.grad.at[self.at(nxt, rest)], self.got.at[i, rest], dev)

    def relay1(self):
        for i, d in enumerate((1, 3)):
            nxt = lax.rem(self.f + d, 4)
            dev = self.who(nxt, self.s, self.y)
            self.live[i].wait_recv()

            @pl.loop(0, 4)
            def _(k):
                a, b = lax.div(k, 2), lax.rem(k, 2)
                own = self.grad[(*self.at(nxt, 2 * i + a), b)].astype(F32)
                self.near[i, a, b] = (own + self.near[i, a, b].astype(F32)).astype(BF16)

            self.copy(4 + i, self.near.at[i], self.got.at[i, pl.ds(2 * i, 2)], dev)

    def start2(self):
        for n in (2, 3, 4, 5):
            self.live[n].wait_recv()

        @pl.loop(0, 8)
        def _(k):
            a, b = lax.div(k, 2), lax.rem(k, 2)
            own = self.grad[self.mine(a, b)].astype(F32)
            total = own + self.got[0, a, b].astype(F32) + self.got[1, a, b].astype(F32)
            self.grad[self.mine(a, b)] = total.astype(BF16)

        for i, d in enumerate((1, 3)):
            dev = self.who(self.f, lax.rem(self.s + d, 4), self.y)
            self.copy(6 + i, self.grad.at[self.mine(lax.rem(self.s + 2, 4), i)], self.near2.at[i], dev)
        for i, d in enumerate((1, 3)):
            nxt = lax.rem(self.s + d, 4)
            dev = self.who(self.f, nxt, self.y)
            self.copy(8 + i, self.grad.at[self.mine(nxt, 1 - i)], self.got2.at[i, 1 - i], dev)

    def relay2(self):
        for i, d in enumerate((1, 3)):
            nxt = lax.rem(self.s + d, 4)
            dev = self.who(self.f, nxt, self.y)
            self.live[6 + i].wait_recv()
            own = self.grad[self.mine(nxt, i)].astype(F32)
            self.near2[i] = (own + self.near2[i].astype(F32)).astype(BF16)
            self.copy(10 + i, self.near2.at[i], self.got2.at[i, i], dev)

    def start3(self):
        for n in (8, 9, 10, 11):
            self.live[n].wait_recv()
        for b in range(2):
            own = self.grad[self.mine(self.s, b)].astype(F32)
            total = own + self.got2[0, b].astype(F32) + self.got2[1, b].astype(F32)
            self.grad[self.mine(self.s, b)] = total.astype(BF16)
        other = 1 - self.y
        self.copy(12, self.grad.at[self.mine(self.s, other)], self.last, self.who(self.f, self.s, other))

    def finish(self):
        self.live[12].wait_recv()
        return self.grad[self.mine(self.s, self.y)].astype(F32) + self.last[...].astype(F32)

    def drain(self):
        for c in self.live.values():
            c.wait_send()


def heads_place():
    g = lax.axis_index("heads")
    y, core = lax.div(g, 2), lax.rem(g, 2)
    return g, y * 2 + 1 - core, (1 - y) * 2 + core, (1 - y) * 2 + 1 - core


def sum_scratch(rows, cols):
    return [
        pltpu.VMEM((2, rows, cols), BF16),
        pltpu.VMEM((rows, cols), BF16),
        pltpu.SemaphoreType.DMA((4,)),
        pltpu.SemaphoreType.DMA((4,)),
    ]


class HeadsSum:
    def __init__(self, parts, rows, refs):
        self.parts, self.rows = parts, rows
        self.near, self.far, self.send, self.recv = refs
        self.live = {}
        self.dp = lax.axis_index("dp")
        self.g, self.mate, self.over, self.over_mate = heads_place()

    def send_near(self, slot):
        quarter = (self.over_mate, self.mate)[slot]
        c = remote(self.parts.at[quarter], self.near.at[slot], self.send.at[slot], self.recv.at[slot], (self.dp, self.mate))
        c.start()
        self.live[slot] = c

    def relay(self):
        self.live[0].wait_recv()
        half = self.rows // 2
        for c in range(2):

            @pl.loop(0, half // 16)
            def _(k):
                at = pl.ds(pl.multiple_of(c * half + 16 * k, 16), 16)
                total = self.near[0, at].astype(F32) + self.parts[self.over, at].astype(F32)
                self.near[0, at] = total.astype(BF16)

            at = pl.ds(c * half, half)
            copy = remote(
                self.near.at[0, at], self.far.at[at], self.send.at[2 + c], self.recv.at[2 + c], (self.dp, self.over)
            )
            copy.start()
            self.live[2 + c] = copy

    def arrive(self, c):
        if c == 0:
            self.live[1].wait_recv()
        self.live[2 + c].wait_recv()

    def total(self, *at):
        return (
            self.parts[(self.g, *at)].astype(F32) + self.near[(1, *at)].astype(F32) + self.far[at].astype(F32)
        )

    def drain(self):
        for c in self.live.values():
            c.wait_send()


class HeadsGather:
    def __init__(self, whole, send, recv):
        self.whole, self.send_sem, self.recv_sem = whole, send, recv
        self.live = {}
        self.dp = lax.axis_index("dp")
        self.g, self.mate, self.over, self.over_mate = heads_place()

    def copy(self, n, quarter, c, dev):
        ref = self.whole.at[quarter, pl.ds(64 * c, 64)]
        copy = remote(ref, ref, self.send_sem.at[n], self.recv_sem.at[n], (self.dp, dev))
        copy.start()
        self.live[n] = copy

    def send(self, c):
        self.copy(c, self.g, c, self.over)
        self.copy(2 + c, self.g, c, self.mate)

    def chip_ready(self):
        for c in range(2):
            self.live[2 + c].wait_recv()

    def forward(self):
        for c in range(2):
            self.live[c].wait_recv()
            self.copy(4 + c, self.over, c, self.mate)

    def all_ready(self):
        for c in range(2):
            self.live[4 + c].wait_recv()

    def drain(self):
        for c in self.live.values():
            c.wait_send()


def spread_rows(flat, start, per_row, block):
    rows, cols = block.shape
    for c in range(cols // 128):
        flat[pl.ds(start + c, rows, per_row), :] = block[:, c * 128 : (c + 1) * 128]


def place_piece(item, total, flat):
    if item == QO:
        for c in range(2):
            spread_rows(flat, c, 2, total[40 * c : 40 * c + 40])
        for c in range(10):
            spread_rows(flat, 592 + c, 10, total[80 + 8 * c : 88 + 8 * c])
    elif item == KK:
        spread_rows(flat, 80, 2, total)
    elif item == VV:
        spread_rows(flat, 336, 2, total)
    elif item == DN:
        spread_rows(flat, 1232, 10, total[0:28])
    else:
        first = 0 if item == GU1 else 5
        spread_rows(flat, 672 + first, 7, total[0:40])
        spread_rows(flat, 952 + first, 7, total[40:80])


def greet():
    z, x, y, g = place()
    dp = lax.axis_index("dp")
    _, mate, over, _ = heads_place()
    partners = [
        (dp, mate),
        (dp, over),
        device_at(lax.rem(z + 1, 4), x, y, g),
        device_at(lax.rem(z + 3, 4), x, y, g),
        device_at(z, lax.rem(x + 1, 4), y, g),
        device_at(z, lax.rem(x + 3, 4), y, g),
        device_at(z, x, 1 - y, g),
    ]
    barrier = pltpu.get_barrier_semaphore()
    for dev in partners:
        pl.semaphore_signal(barrier, inc=1, device_id=dev, device_id_type=MESH_ID)
    pl.semaphore_wait(barrier, len(partners))


def rows_at(first, k, size):
    return pl.ds(pl.multiple_of(first + size * k, size), size)


def layer_scratch():
    quarters = lambda cols, kind: pltpu.VMEM((4, 128, cols), kind)
    plain = dict(
        states=quarters(D, BF16),
        patches=pltpu.VMEM((128, DG), BF16),
        cot=quarters(D, BF16),
        wq=pltpu.VMEM((D, 256), BF16),
        wk=pltpu.VMEM((DG, 256), BF16),
        wv=pltpu.VMEM((DG, 256), BF16),
        wo=pltpu.VMEM((256, D), BF16),
        wg=pltpu.VMEM((D, UNITS), BF16),
        wu=pltpu.VMEM((D, UNITS), BF16),
        wd=pltpu.VMEM((UNITS, D), BF16),
        loads=pltpu.SemaphoreType.DMA((10,)),
        normed=quarters(D, BF16),
        query=quarters(256, F32),
        key=pltpu.VMEM((128, 256), F32),
        keyn=pltpu.VMEM((128, 256), BF16),
        value=pltpu.VMEM((128, 256), BF16),
        att=quarters(256, BF16),
        part1=quarters(D, BF16),
        part2=quarters(D, BF16),
        part4=pltpu.VMEM((4, 32, DG), BF16),
        res=pltpu.VMEM((128, D), F32),
        resg=pltpu.VMEM((128, D), F32),
        nh=quarters(D, BF16),
        rh=quarters(D, BF16),
        turned=pltpu.VMEM((D, 512), BF16),
        attt=pltpu.VMEM((256, 512), BF16),
        hgrad=pltpu.VMEM((512, UNITS), F32),
        gg=pltpu.VMEM((512, UNITS), BF16),
        ug=pltpu.VMEM((512, UNITS), BF16),
        hid=pltpu.VMEM((512, UNITS), BF16),
        qgrad=quarters(256, BF16),
        keyg=pltpu.VMEM((128, 256), F32),
        valg=pltpu.VMEM((128, 256), F32),
        kg=pltpu.VMEM((128, 256), BF16),
        vg=pltpu.VMEM((128, 256), BF16),
        down=pltpu.VMEM((120, D), F32),
        g1s=pltpu.SemaphoreType.DMA((6,)),
        g1r=pltpu.SemaphoreType.DMA((6,)),
        g2s=pltpu.SemaphoreType.DMA((6,)),
        g2r=pltpu.SemaphoreType.DMA((6,)),
    )
    sums = [sum_scratch(128, D), sum_scratch(128, D), sum_scratch(128, D), sum_scratch(32, DG)]
    jobs = [scatter_scratch(i) for i in range(len(PIECES))]
    return plain, sums, jobs


class Refs:
    pass


def layer_kernel(*refs):
    (lengths, again, fgain, states_h, patches_h, cot_h, wq_h, wk_h, wv_h, wo_h, wg_h, wu_h, wd_h,
     flat, out_bytes, out_patches) = refs[:16]
    plain, sums, jobs = layer_scratch()
    rest = list(refs[16:])
    r = Refs()
    for name in plain:
        setattr(r, name, rest.pop(0))
    sum_refs = [[rest.pop(0) for _ in s] for s in sums]
    jobs = [Scatter(i, [rest.pop(0) for _ in s]) for i, s in enumerate(jobs)]
    g, mate, over, over_mate = heads_place()
    own_pair = lax.div(g, 2)

    moves = {}
    order = [
        ("patches", patches_h), ("wk", wk_h), ("wv", wv_h), ("states", states_h), ("wq", wq_h), ("wo", wo_h),
        ("cot", cot_h), ("wd", wd_h), ("wg", wg_h), ("wu", wu_h),
    ]
    for i, (name, src) in enumerate(order):
        moves[name] = pltpu.make_async_copy(src, getattr(r, name), r.loads.at[i])
        moves[name].start()
    greet()

    sum1 = HeadsSum(r.part1, 128, sum_refs[0])
    sum2 = HeadsSum(r.part2, 128, sum_refs[1])
    sum3 = HeadsSum(r.part1, 128, sum_refs[2])
    sum4 = HeadsSum(r.part4, 32, sum_refs[3])
    gather1 = HeadsGather(r.nh, r.g1s, r.g1r)
    gather2 = HeadsGather(r.rh, r.g2s, r.g2r)

    moves["patches"].wait()
    moves["wk"].wait()
    key = nn(r.patches[...], r.wk[...])
    r.key[...] = key
    for h in range(2):
        cols = slice(HEAD * h, HEAD * h + HEAD)
        one = key[:, cols]
        r.keyn[:, cols] = (one * inverse_rms(one)).astype(BF16)
    moves["wv"].wait()
    r.value[...] = nn(r.patches[...], r.wv[...]).astype(BF16)
    earlier = lax.broadcasted_iota(jnp.int32, (128, 128), 0) < lax.broadcasted_iota(jnp.int32, (128, 128), 1)
    spans = jnp.broadcast_to(lengths[...].astype(F32), (16, 128)).astype(BF16)
    starts = nn(spans, earlier.astype(F32).astype(BF16))[0:1]

    def head_probabilities(qi, h):
        cols = slice(HEAD * h, HEAD * h + HEAD)
        full = r.query[qi, :, cols]
        inverse = inverse_rms(full)
        query = (full * inverse).astype(BF16)
        scores = score_scale * nt(query, r.keyn[:, cols])
        position = (lax.broadcasted_iota(jnp.int32, (128, 128), 0) + qi * 128).astype(F32)
        weights = jnp.where(starts <= position, jnp.exp(scores), 0.0)
        return full, inverse, query, weights / jnp.sum(weights, axis=-1, keepdims=True)

    moves["states"].wait()
    moves["wq"].wait()
    moves["wo"].wait()

    def attend(qi):
        @pl.loop(0, 4)
        def _(k):
            at = rows_at(0, k, 32)
            x = r.states[qi, at].astype(F32)
            r.normed[qi, at] = (x * inverse_rms(x) * again[...]).astype(BF16)

        r.query[qi] = nn(r.normed[qi], r.wq[...])
        for h in range(2):
            cols = slice(HEAD * h, HEAD * h + HEAD)
            prob = head_probabilities(qi, h)[3]
            r.att[qi, :, cols] = nn(prob.astype(BF16), r.value[:, cols]).astype(BF16)
        for lo, hi in WIDE_TILES:
            r.part1[qi, :, lo:hi] = nn(r.att[qi], r.wo[:, lo:hi]).astype(BF16)

    attend(over_mate)
    sum1.send_near(0)
    attend(mate)
    sum1.send_near(1)
    attend(over)
    sum1.relay()
    attend(g)

    moves["cot"].wait()
    moves["wd"].wait()

    @pl.loop(0, 2)
    def _(p):
        at = rows_at(0, p, 256)
        cot = r.cot[pl.ds(2 * p, 2)].reshape(256, D)
        for lo, hi in UNIT_TILES:
            r.hgrad[at, lo:hi] = nt(cot, r.wd[lo:hi, :])

    for c in range(2):
        sum1.arrive(c)

        @pl.loop(0, 2)
        def _(k):
            at = rows_at(64 * c, k, 32)
            res = r.states[g, at].astype(F32) + sum1.total(at)
            r.res[at] = res
            r.nh[g, at] = (res * inverse_rms(res) * fgain[...]).astype(BF16)

        gather1.send(c)
    sum1.drain()
    moves["wg"].wait()
    moves["wu"].wait()

    def feed(p):
        at = rows_at(0, p, 256)
        normed = r.nh[pl.ds(2 * p, 2)].reshape(256, D)
        for lo, hi in UNIT_TILES:
            gate = nn(normed, r.wg[:, lo:hi])
            up = nn(normed, r.wu[:, lo:hi])
            back = r.hgrad[at, lo:hi]
            sigma = jax.nn.sigmoid(gate)
            active = gate * sigma
            r.hid[at, lo:hi] = (active * up).astype(BF16)
            r.gg[at, lo:hi] = (back * up * (sigma * (1.0 + gate * (1.0 - sigma)))).astype(BF16)
            r.ug[at, lo:hi] = (back * active).astype(BF16)
        for lo, hi in WIDE_TILES:
            part = nt(r.gg[at], r.wg[lo:hi, :]) + nt(r.ug[at], r.wu[lo:hi, :])
            r.part2[pl.ds(2 * p, 2), :, lo:hi] = part.astype(BF16).reshape(2, 128, hi - lo)

    gather1.chip_ready()
    feed(own_pair)
    sum2.send_near(1)
    gather1.forward()
    gather1.all_ready()
    feed(1 - own_pair)
    sum2.send_near(0)
    sum2.relay()

    for q in range(4):
        r.turned[:, 128 * q : 128 * q + 128] = r.nh[q].T

    @pl.loop(0, 8)
    def _(c):
        rows = r.turned[rows_at(0, c, 160)]
        z, x = lax.div(c, 2), 2 * lax.rem(c, 2)
        for grad, row in ((r.gg, 0), (r.ug, 40)):
            for job, lo, hi in ((GU1, 0, 256), (GU1, 256, 512), (GU1, 512, 640), (GU2, 640, 896)):
                got = nn(rows, grad[:, lo:hi])
                col = lo if job == GU1 else 0
                for j in range(4):
                    jobs[job].grad[z, x + j // 2, j % 2, row : row + 40, col : col + hi - lo] = got[
                        40 * j : 40 * j + 40
                    ].astype(BF16)

    jobs[GU1].start1()
    jobs[GU2].start1()

    for c in range(2):
        sum2.arrive(c)

        @pl.loop(0, 2)
        def _(k):
            at = rows_at(64 * c, k, 32)
            res = r.res[at]
            grad = r.cot[g, at].astype(F32) + norm_backward(res, inverse_rms(res), sum2.total(at) * fgain[...])
            r.resg[at] = grad
            r.rh[g, at] = grad.astype(BF16)

        gather2.send(c)
    sum2.drain()

    for q in range(4):
        r.turned[0:UNITS, 128 * q : 128 * q + 128] = r.hid[128 * q : 128 * q + 128].T
    r.down[112:120] = jnp.zeros((8, D), F32)

    @pl.loop(0, 8)
    def _(c):
        rows = r.turned[rows_at(0, c, 112)]
        for lo, hi in WIDE_TILES:
            r.down[0:112, lo:hi] = nn(rows, r.cot[:, :, lo:hi].reshape(512, hi - lo))
        z, x = lax.div(c, 2), 2 * lax.rem(c, 2)
        for j in range(4):
            jobs[DN].grad[z, x + j // 2, j % 2] = r.down[28 * j : 28 * j + 32].astype(BF16)

    jobs[DN].start1()

    r.keyg[...] = jnp.zeros((128, 256), F32)
    r.valg[...] = jnp.zeros((128, 256), F32)

    def attend_back(qi):
        agrad = nt(r.rh[qi], r.wo[...]).astype(BF16)
        for h in range(2):
            cols = slice(HEAD * h, HEAD * h + HEAD)
            full, inverse, query, prob = head_probabilities(qi, h)
            back = nt(agrad[:, cols], r.value[:, cols])
            inner = jnp.sum(prob * back, axis=-1, keepdims=True)
            score = (score_scale * prob * (back - inner)).astype(BF16)
            grad = nn(score, r.keyn[:, cols])
            r.keyg[:, cols] += tn(score, query)
            r.valg[:, cols] += tn(prob.astype(BF16), agrad[:, cols])
            r.qgrad[qi, :, cols] = norm_backward(full, inverse, grad).astype(BF16)

    attend_back(g)
    gather2.chip_ready()
    attend_back(mate)
    gather2.forward()
    jobs[GU1].relay1()
    jobs[GU2].relay1()
    attend_back(over)
    gather2.all_ready()
    attend_back(over_mate)
    for h in range(2):
        cols = slice(HEAD * h, HEAD * h + HEAD)
        full = r.key[:, cols]
        r.kg[:, cols] = norm_backward(full, inverse_rms(full), r.keyg[:, cols]).astype(BF16)
    r.vg[...] = r.valg[...].astype(BF16)

    @pl.loop(0, 32)
    def _(p):
        rows = r.patches[:, rows_at(0, p, 128)].T
        at = (lax.div(p, 8), lax.rem(lax.div(p, 2), 4), lax.rem(p, 2))
        jobs[KK].grad[at] = nn(rows, r.kg[...]).astype(BF16)
        jobs[VV].grad[at] = nn(rows, r.vg[...]).astype(BF16)

    jobs[KK].start1()
    jobs[VV].start1()
    jobs[DN].relay1()

    for q in range(4):
        r.turned[:, 128 * q : 128 * q + 128] = r.normed[q].T
        r.attt[:, 128 * q : 128 * q + 128] = r.att[q].T
    for half in range(2):
        for lo, hi in ((0, 256), (256, 512), (512, 640)):
            cols = slice(640 * half + lo, 640 * half + hi)
            r.hgrad[256 * half : 256 * half + 256, lo:hi] = nn(
                r.attt[...], r.rh[:, :, cols].reshape(512, hi - lo)
            )

    @pl.loop(0, 4)
    def _(c):
        got = nn(r.turned[rows_at(0, c, 320)], r.qgrad[...].reshape(512, 256))
        for j in range(8):
            mine = got[40 * j : 40 * j + 40]
            halves = [r.hgrad[rows_at(256 * half + 8 * j, c * 8, 8), 0:640] for half in range(2)]
            blocks = [mine[:, :128], mine[:, 128:]]
            blocks += [m[:, 128 * n : 128 * n + 128] for m in halves for n in range(5)]
            jobs[QO].grad[c, j // 2, j % 2] = jnp.concatenate(blocks, axis=0).astype(BF16)

    jobs[QO].start1()

    @pl.loop(0, 2)
    def _(p):
        grad = r.qgrad[pl.ds(2 * p, 2)].reshape(256, 256)
        for lo, hi in WIDE_TILES:
            r.part1[pl.ds(2 * p, 2), :, lo:hi] = nt(grad, r.wq[lo:hi, :]).astype(BF16).reshape(2, 128, hi - lo)

    sum3.send_near(0)
    sum3.send_near(1)

    @pl.loop(0, 16)
    def _(n):
        at = rows_at(0, n, 256)
        part = nt(r.kg[...], r.wk[at]) + nt(r.vg[...], r.wv[at])
        r.part4[:, :, at] = part.astype(BF16).reshape(4, 32, 256)

    sum4.send_near(0)
    sum4.send_near(1)
    sum3.relay()
    sum4.relay()
    for n in (GU1, GU2, DN):
        jobs[n].start2()
    for n in (KK, VV, QO):
        jobs[n].relay1()
    for n in (GU1, GU2, DN):
        jobs[n].relay2()

    for c in range(2):
        sum3.arrive(c)

        @pl.loop(0, 2)
        def _(k):
            at = rows_at(64 * c, k, 32)
            x = r.states[g, at].astype(F32)
            grad = r.resg[at] + norm_backward(x, inverse_rms(x), sum3.total(at) * again[...])
            out_bytes[at] = grad.astype(BF16)

    for c in range(2):
        sum4.arrive(c)

        @pl.loop(0, 4)
        def _(k):
            at = (pl.ds(16 * c, 16), rows_at(0, k, 1024))
            out_patches[at] = sum4.total(*at).astype(BF16)

    for n in (KK, VV, QO):
        jobs[n].start2()
    for n in (GU1, GU2, DN):
        jobs[n].start3()
    for n in (KK, VV, QO):
        jobs[n].relay2()
    for n in (GU1, GU2, DN):
        place_piece(n, jobs[n].finish(), flat)
    for n in (KK, VV, QO):
        jobs[n].start3()
    for n in (KK, VV, QO):
        place_piece(n, jobs[n].finish(), flat)
    for item in (*jobs, sum3, sum4, gather1, gather2):
        item.drain()


def shards(
    byte_states,
    patch_states,
    patch_lengths,
    cotangent,
    attention_gain,
    feedforward_gain,
    query_weight,
    key_weight,
    value_weight,
    output_weight,
    gate_weight,
    up_weight,
    down_weight,
    adam_first,
    adam_second,
):
    row_count = byte_states.shape[0]
    piece_count = lax.axis_size("dp")
    plain, sums, jobs = layer_scratch()
    vmem = pl.BlockSpec(memory_space=pltpu.VMEM)
    summed, input_grad, patch_grad = pl.pallas_call(
        layer_kernel,
        out_shape=(
            jax.ShapeDtypeStruct((FLAT, 128), F32),
            jax.ShapeDtypeStruct((128, D), BF16),
            jax.ShapeDtypeStruct((32, DG), BF16),
        ),
        in_specs=[vmem] * 3 + [pl.BlockSpec(memory_space=pl.ANY)] * 10,
        out_specs=(vmem, vmem, vmem),
        scratch_shapes=[*plain.values(), *(s for group in (*sums, *jobs) for s in group)],
        compiler_params=pltpu.CompilerParams(
            collective_id=0, has_side_effects=True, vmem_limit_bytes=63 * MIB
        ),
    )(
        patch_lengths,
        attention_gain.reshape(1, D),
        feedforward_gain.reshape(1, D),
        byte_states.reshape(4, 128, D),
        patch_states,
        cotangent.reshape(4, 128, D),
        query_weight,
        key_weight,
        value_weight,
        output_weight,
        gate_weight,
        up_weight,
        down_weight,
    )
    gradient = summed * float(row_count * piece_count) ** (-0.5)
    new_first = beta_first * adam_first.reshape(FLAT, 128) + (1.0 - beta_first) * gradient
    new_second = beta_second * adam_second.reshape(FLAT, 128) + (1.0 - beta_second) * gradient * gradient
    adam_step = new_first / bias_first / (jnp.sqrt(new_second / bias_second) + adam_epsilon)
    return (
        input_grad,
        patch_grad,
        new_first.reshape(1, -1),
        new_second.reshape(1, -1),
        adam_step.reshape(1, -1),
    )


def solution(mesh):
    placed = (
        P("dp", None),
        P("dp", None),
        P("dp", None),
        P("dp", None),
        P(),
        P(),
        P(None, "heads"),
        P(None, "heads"),
        P(None, "heads"),
        P("heads", None),
        P(None, "heads"),
        P(None, "heads"),
        P("heads", None),
        P("heads", "dp"),
        P("heads", "dp"),
    )
    return jax.shard_map(
        shards,
        mesh=mesh,
        in_specs=placed,
        out_specs=(
            P(("dp", "heads"), None),
            P(("dp", "heads"), None),
            P("heads", "dp"),
            P("heads", "dp"),
            P("heads", "dp"),
        ),
        check_vma=False,
    )
```

time: 282 us -> 131 us (0.46)
  waiting for transfers between devices: 73.3 us -> 0 us
  matrix products: 45.7 us -> 0 us
  Pallas kernels: 87.4 us -> 120 us
  other arithmetic: 35.3 us -> 6.42 us
  local copies, waits for them, and re-layouts: 24.5 us -> 4.1 us
  between operations: 14.7 us -> 0.68 us
    dot_general x26 -> x0, matrix products: 45.7 us -> none  [the longest x7 13.7 us: matmul_left_t(): lax.dot_general(left, right, (((0,), (0,)), ((), ())), preferred_element_...]
    reduce_scatter x4 -> x0, waiting for transfers between devices: 42.6 us -> none  [the longest x1 21.3 us: shards(): lax.psum_scatter(attention_part.astype(jnp.bfloat16), 'heads', scatter_di...]
    pallas_call x1, Pallas kernels: 87.4 us -> 120 us  [shards(): pl.pallas_call(layer_kernel, out_shape=(jax.ShapeDtypeStruct((FLAT, 128),...]
    all_gather x2 -> x0, waiting for transfers between devices: 30.6 us -> none  [the longest x1 23.7 us: shards(): normed_hidden = lax.all_gather(normed_share, 'heads', axis=0, tiled=True)]
    convert_element_type x8 -> x0, other arithmetic: 12 us -> none  [the longest x1 2.99 us: shards(): byte_float = byte_states.astype(jnp.float32)]
    convert_element_type x3 -> x0, local copies, waits for them, and re-layouts: 9.2 us -> none  [the longest x1 4.12 us: shards(): grad_down.reshape(32, 28, -1).astype(BF16)]
    reduce_sum x6 -> x0, other arithmetic: 7.23 us -> none  [the longest x2 3.29 us: norm_backward(): jnp.mean(inputs * inputs, axis=-1, keepdims=True) + norm_epsilon]
    dot_general x3 -> x0, local copies, waits for them, and re-layouts: 6.02 us -> none  [the longest x2 5.03 us: matmul_left_t(): lax.dot_general(left, right, (((0,), (0,)), ((), ())), preferred_element_...]
  transfers between devices with their start and end apart: 6 -> 0, of which waited for: 4 -> 0; matrix products, arithmetic and copies ran while one was open for 21% -> 0% of each run, Pallas kernels for 31% -> 0%
where the time goes in v2:
time: 131 us
  Pallas kernels  120 us (92%)
  other arithmetic  6.42 us (5%)
  local copies, waits for them, and re-layouts  4.1 us (3%)
    pallas_call x1, Pallas kernels, shards(): pl.pallas_call(layer_kernel, out_shape=(jax.ShapeDtypeStruct((FLAT, 128),...  120 us
    div x1, other arithmetic, shards(): new_first / bias_first / (jnp.sqrt(new_second / bias_second) + adam_epsilon)  3.02 us

profile of v2, /device:TPU:0, one launch (start us, length us, event | category | flops | bytes accessed | tf_op | source)
XLA Modules:
  0.0 130.8 jit_solution(7433289103282536084)
XLA Ops:
  0.6 0.0 copy-start
  0.6 1.4 %reshape.37.refs_1_ = f32[1,1280]{1,0:T(1,128)} reshape(f32[1280]{0:T(1024)} %param.19) | data formatting | bytes 10240 | tf_op jit(solution)/shard_map/reshape | solution.py:722
  2.0 1.3 reshape.38.refs_2_
  3.3 1.8 %broadcast_multiply_fusion.1 = f32[1,193536]{1,0:T(1,128)S(1)} fusion(f32[1,193536]{1,0:T(1,128)} %param.28), kind=kLoop, calls=%fused_computation.4 | loop fusion | flops 193536 | bytes 1548288 | tf_op jit(solution)/shard_map/mul | solution.py:736
  5.1 0.0 copy-done
  5.1 1.6 %broadcast_multiply_fusion = f32[1,193536]{1,0:T(1,128)} fusion(f32[1,193536]{1,0:T(1,128)S(1)} %copy-done), kind=kLoop, calls=%fused_computation.3 | loop fusion | flops 193536 | bytes 1548288 | tf_op jit(solution)/shard_map/mul | solution.py:737
  6.7 119.6 %shard_map.182 = (f32[1512,128]{1,0:T(8,128)}, bf16[128,1280]{1,0:T(8,128)(2,1)}, bf16[32,4096]{1,0:T(8,128)(2,1)}) custom-call(s32[1,128]{1,0:T(1,128)} %refs_0_.1, f32[1,1280]{1,0:T(1,128)} %reshape.37.refs_1_, f32[1,1280]{1,0:T(1,128)} %reshape.38.refs_2_, bf16[4,128,1280]{2,1,0:T(8,128)(2,1)} %bitcast.9, bf16[128,4096]{1,0:T(8,128)(2,1)} %refs_4_.1, ...), custom_call_target="tpu_custom_call" | custom-call | tf_op jit(solution)/shard_map/pallas_call | solution.py:707
  126.4 0.0 copy-start.1
  126.4 0.0 copy-start.2
  126.4 3.0 %add_divide_fusion = (f32[1512,128]{1,0:T(8,128)}, f32[1512,128]{1,0:T(8,128)}, f32[1512,128]{1,0:T(8,128)}) fusion(f32[1512,128]{1,0:T(8,128)} %bitcast.8, f32[1512,128]{1,0:T(8,128)} %get-tuple-element.10, f32[1512,128]{1,0:T(8,128)S(1)} %bitcast.7), kind=kLoop, calls=%fused_computation | loop fusion | flops 1935360 | bytes 4644864 | tf_op jit(solution)/shard_map/div | solution.py:738
  129.4 0.0 copy-done.1
  129.4 0.7 copy.22
  130.1 0.0 copy-done.2
  130.1 0.7 copy.23
Async XLA Ops:
  0.6 4.5 %copy-start = (f32[1,193536]{1,0:T(1,128)S(1)}, f32[1,193536]{1,0:T(1,128)}, u32[]{:S(2)}) copy-start(f32[1,193536]{1,0:T(1,128)} %param.29) | copy-start | bytes 2322436
  126.4 3.0 %copy-start.1 = (bf16[128,1280]{1,0:T(8,128)(2,1)S(1)}, bf16[128,1280]{1,0:T(8,128)(2,1)}, u32[]{:S(2)}) copy-start(bf16[128,1280]{1,0:T(8,128)(2,1)} %get-tuple-element.19) | copy-start | bytes 983044
  126.4 3.8 %copy-start.2 = (bf16[32,4096]{1,0:T(8,128)(2,1)S(1)}, bf16[32,4096]{1,0:T(8,128)(2,1)}, u32[]{:S(2)}) copy-start(bf16[32,4096]{1,0:T(8,128)(2,1)} %get-tuple-element.20) | copy-start | bytes 786436

commit v3 on v2

--- a/solution.py
+++ b/solution.py
@@ -198,6 +198,15 @@
     ]
 
 
+def pair_scratch():
+    return [
+        pltpu.VMEM((2, 128, D), BF16),
+        pltpu.VMEM((2, 128, D), BF16),
+        pltpu.SemaphoreType.DMA((6,)),
+        pltpu.SemaphoreType.DMA((6,)),
+    ]
+
+
 class HeadsSum:
     def __init__(self, parts, rows, refs):
         self.parts, self.rows = parts, rows
@@ -245,35 +254,65 @@
             c.wait_send()
 
 
-class HeadsGather:
+class PairSum:
+    def __init__(self, parts, refs):
+        self.parts = parts
+        self.near, self.far, self.send, self.recv = refs
+        self.live = {}
+        self.dp = lax.axis_index("dp")
+        self.g, self.mate, self.over, _ = heads_place()
+        self.core = lax.rem(self.g, 2)
+
+    def copy(self, n, src, dst, dev):
+        c = remote(src, dst, self.send.at[n], self.recv.at[n], (self.dp, dev))
+        c.start()
+        self.live[n] = c
+
+    def send_near(self, b):
+        self.copy(b, self.parts.at[2 * b + 1 - self.core], self.near.at[b], self.mate)
+
+    def relay(self, b):
+        self.live[b].wait_recv()
+        for c in range(2):
+
+            @pl.loop(0, 4)
+            def _(k):
+                at = pl.ds(pl.multiple_of(c * 64 + 16 * k, 16), 16)
+                total = self.near[b, at].astype(F32) + self.parts[2 * b + self.core, at].astype(F32)
+                self.near[b, at] = total.astype(BF16)
+
+            at = pl.ds(c * 64, 64)
+            self.copy(2 + 2 * b + c, self.near.at[b, at], self.far.at[b, at], self.over)
+
+    def arrive(self, b, c):
+        self.live[2 + 2 * b + c].wait_recv()
+
+    def total(self, b, at):
+        return self.near[b, at].astype(F32) + self.far[b, at].astype(F32)
+
+    def drain(self):
+        for c in self.live.values():
+            c.wait_send()
+
+
+class CoreSwap:
     def __init__(self, whole, send, recv):
         self.whole, self.send_sem, self.recv_sem = whole, send, recv
         self.live = {}
         self.dp = lax.axis_index("dp")
-        self.g, self.mate, self.over, self.over_mate = heads_place()
-
-    def copy(self, n, quarter, c, dev):
-        ref = self.whole.at[quarter, pl.ds(64 * c, 64)]
-        copy = remote(ref, ref, self.send_sem.at[n], self.recv_sem.at[n], (self.dp, dev))
+        self.g, self.mate, _, _ = heads_place()
+        self.core = lax.rem(self.g, 2)
+
+    def give(self, b, c):
+        n = 2 * b + c
+        ref = self.whole.at[2 * b + self.core, pl.ds(64 * c, 64)]
+        copy = remote(ref, ref, self.send_sem.at[n], self.recv_sem.at[n], (self.dp, self.mate))
         copy.start()
         self.live[n] = copy
 
-    def send(self, c):
-        self.copy(c, self.g, c, self.over)
-        self.copy(2 + c, self.g, c, self.mate)
-
-    def chip_ready(self):
+    def take(self, b):
         for c in range(2):
-            self.live[2 + c].wait_recv()
-
-    def forward(self):
-        for c in range(2):
-            self.live[c].wait_recv()
-            self.copy(4 + c, self.over, c, self.mate)
-
-    def all_ready(self):
-        for c in range(2):
-            self.live[4 + c].wait_recv()
+            self.live[2 * b + c].wait_recv()
 
     def drain(self):
         for c in self.live.values():
@@ -350,28 +389,27 @@
         part1=quarters(D, BF16),
         part2=quarters(D, BF16),
         part4=pltpu.VMEM((4, 32, DG), BF16),
-        res=pltpu.VMEM((128, D), F32),
-        resg=pltpu.VMEM((128, D), F32),
+        res=pltpu.VMEM((2, 128, D), F32),
+        gain1=pltpu.VMEM((1, D), F32),
+        gain2=pltpu.VMEM((1, D), F32),
         nh=quarters(D, BF16),
         rh=quarters(D, BF16),
         turned=pltpu.VMEM((D, 512), BF16),
-        attt=pltpu.VMEM((256, 512), BF16),
         hgrad=pltpu.VMEM((512, UNITS), F32),
         gg=pltpu.VMEM((512, UNITS), BF16),
         ug=pltpu.VMEM((512, UNITS), BF16),
-        hid=pltpu.VMEM((512, UNITS), BF16),
         qgrad=quarters(256, BF16),
         keyg=pltpu.VMEM((128, 256), F32),
         valg=pltpu.VMEM((128, 256), F32),
         kg=pltpu.VMEM((128, 256), BF16),
         vg=pltpu.VMEM((128, 256), BF16),
         down=pltpu.VMEM((120, D), F32),
-        g1s=pltpu.SemaphoreType.DMA((6,)),
-        g1r=pltpu.SemaphoreType.DMA((6,)),
-        g2s=pltpu.SemaphoreType.DMA((6,)),
-        g2r=pltpu.SemaphoreType.DMA((6,)),
+        g1s=pltpu.SemaphoreType.DMA((4,)),
+        g1r=pltpu.SemaphoreType.DMA((4,)),
+        g2s=pltpu.SemaphoreType.DMA((4,)),
+        g2r=pltpu.SemaphoreType.DMA((4,)),
     )
-    sums = [sum_scratch(128, D), sum_scratch(128, D), sum_scratch(128, D), sum_scratch(32, DG)]
+    sums = [pair_scratch(), pair_scratch(), sum_scratch(128, D), sum_scratch(32, DG)]
     jobs = [scatter_scratch(i) for i in range(len(PIECES))]
     return plain, sums, jobs
 
@@ -388,10 +426,12 @@
     r = Refs()
     for name in plain:
         setattr(r, name, rest.pop(0))
+    r.hid = r.wd.at[0:512, 0:UNITS]
+    r.attt = r.wd.at[512:768, 0:512]
     sum_refs = [[rest.pop(0) for _ in s] for s in sums]
     jobs = [Scatter(i, [rest.pop(0) for _ in s]) for i, s in enumerate(jobs)]
-    g, mate, over, over_mate = heads_place()
-    own_pair = lax.div(g, 2)
+    g, _, _, _ = heads_place()
+    core = lax.rem(g, 2)
 
     moves = {}
     order = [
@@ -400,18 +440,23 @@
     ]
     for i, (name, src) in enumerate(order):
         moves[name] = pltpu.make_async_copy(src, getattr(r, name), r.loads.at[i])
+    for name in ("patches", "wk", "wv", "states", "wq"):
         moves[name].start()
+    r.gain1[...] = again[...].reshape(1, D)
+    r.gain2[...] = fgain[...].reshape(1, D)
     greet()
 
-    sum1 = HeadsSum(r.part1, 128, sum_refs[0])
-    sum2 = HeadsSum(r.part2, 128, sum_refs[1])
+    sum1 = PairSum(r.part1, sum_refs[0])
+    sum2 = PairSum(r.part2, sum_refs[1])
     sum3 = HeadsSum(r.part1, 128, sum_refs[2])
     sum4 = HeadsSum(r.part4, 32, sum_refs[3])
-    gather1 = HeadsGather(r.nh, r.g1s, r.g1r)
-    gather2 = HeadsGather(r.rh, r.g2s, r.g2r)
+    swap1 = CoreSwap(r.nh, r.g1s, r.g1r)
+    swap2 = CoreSwap(r.rh, r.g2s, r.g2r)
 
     moves["patches"].wait()
     moves["wk"].wait()
+    for name in ("wo", "cot", "wd", "wg", "wu"):
+        moves[name].start()
     key = nn(r.patches[...], r.wk[...])
     r.key[...] = key
     for h in range(2):
@@ -443,7 +488,7 @@
         def _(k):
             at = rows_at(0, k, 32)
             x = r.states[qi, at].astype(F32)
-            r.normed[qi, at] = (x * inverse_rms(x) * again[...]).astype(BF16)
+            r.normed[qi, at] = (x * inverse_rms(x) * r.gain1[...]).astype(BF16)
 
         r.query[qi] = nn(r.normed[qi], r.wq[...])
         for h in range(2):
@@ -453,13 +498,11 @@
         for lo, hi in WIDE_TILES:
             r.part1[qi, :, lo:hi] = nn(r.att[qi], r.wo[:, lo:hi]).astype(BF16)
 
-    attend(over_mate)
-    sum1.send_near(0)
-    attend(mate)
-    sum1.send_near(1)
-    attend(over)
-    sum1.relay()
-    attend(g)
+    for b in range(2):
+        attend(2 * b + 1 - core)
+        sum1.send_near(b)
+        attend(2 * b + core)
+        sum1.relay(b)
 
     moves["cot"].wait()
     moves["wd"].wait()
@@ -471,23 +514,40 @@
         for lo, hi in UNIT_TILES:
             r.hgrad[at, lo:hi] = nt(cot, r.wd[lo:hi, :])
 
-    for c in range(2):
-        sum1.arrive(c)
-
-        @pl.loop(0, 2)
-        def _(k):
-            at = rows_at(64 * c, k, 32)
-            res = r.states[g, at].astype(F32) + sum1.total(at)
-            r.res[at] = res
-            r.nh[g, at] = (res * inverse_rms(res) * fgain[...]).astype(BF16)
-
-        gather1.send(c)
-    sum1.drain()
+    def residual(b):
+        for c in range(2):
+            sum1.arrive(b, c)
+
+            @pl.loop(0, 2)
+            def _(k):
+                at = rows_at(64 * c, k, 32)
+                res = r.states[2 * b + core, at].astype(F32) + sum1.total(b, at)
+                r.res[b, at] = res
+                r.nh[2 * b + core, at] = (res * inverse_rms(res) * r.gain2[...]).astype(BF16)
+
+            swap1.give(b, c)
+
+    def residual_back(b):
+        for c in range(2):
+            sum2.arrive(b, c)
+
+            @pl.loop(0, 2)
+            def _(k):
+                at = rows_at(64 * c, k, 32)
+                res = r.res[b, at]
+                grad = norm_backward(res, inverse_rms(res), sum2.total(b, at) * r.gain2[...])
+                grad = grad + r.cot[2 * b + core, at].astype(F32)
+                r.res[b, at] = grad
+                r.rh[2 * b + core, at] = grad.astype(BF16)
+
+            swap2.give(b, c)
+
+    residual(0)
     moves["wg"].wait()
     moves["wu"].wait()
 
     def feed(p):
-        at = rows_at(0, p, 256)
+        at = slice(256 * p, 256 * p + 256)
         normed = r.nh[pl.ds(2 * p, 2)].reshape(256, D)
         for lo, hi in UNIT_TILES:
             gate = nn(normed, r.wg[:, lo:hi])
@@ -502,61 +562,66 @@
             part = nt(r.gg[at], r.wg[lo:hi, :]) + nt(r.ug[at], r.wu[lo:hi, :])
             r.part2[pl.ds(2 * p, 2), :, lo:hi] = part.astype(BF16).reshape(2, 128, hi - lo)
 
-    gather1.chip_ready()
-    feed(own_pair)
+    def store(ref, at, rows, cols, new, again_):
+        at = (*at, rows, cols)
+        if again_:
+            new = new + ref[at].astype(F32)
+        ref[at] = new.astype(BF16)
+
+    def turn(p):
+        for q in (2 * p, 2 * p + 1):
+            r.turned[:, 128 * q : 128 * q + 128] = r.nh[q].T
+
+    def gate_up_grads(p):
+        @pl.loop(0, 8)
+        def _(c):
+            rows = r.turned[rows_at(0, c, 160), 256 * p : 256 * p + 256]
+            z, x = lax.div(c, 2), 2 * lax.rem(c, 2)
+            for grad, row in ((r.gg, 0), (r.ug, 40)):
+                for job, lo, hi in ((GU1, 0, 256), (GU1, 256, 512), (GU1, 512, 640), (GU2, 640, 896)):
+                    got = nn(rows, grad[256 * p : 256 * p + 256, lo:hi])
+                    col = lo if job == GU1 else 0
+                    for j in range(4):
+                        store(
+                            jobs[job].grad, (z, x + j // 2, j % 2), slice(row, row + 40), slice(col, col + hi - lo),
+                            got[40 * j : 40 * j + 40], p,
+                        )
+
+    def down_grads(p):
+        for q in (2 * p, 2 * p + 1):
+            r.turned[0:UNITS, 128 * q : 128 * q + 128] = r.hid[128 * q : 128 * q + 128].T
+
+        @pl.loop(0, 8)
+        def _(c):
+            rows = r.turned[rows_at(0, c, 112), 256 * p : 256 * p + 256]
+            for lo, hi in WIDE_TILES:
+                r.down[0:112, lo:hi] = nn(rows, r.cot[2 * p : 2 * p + 2, :, lo:hi].reshape(256, hi - lo))
+            z, x = lax.div(c, 2), 2 * lax.rem(c, 2)
+            for j in range(4):
+                store(
+                    jobs[DN].grad, (z, x + j // 2, j % 2), slice(0, 32), slice(0, D), r.down[28 * j : 28 * j + 32], p
+                )
+
+    r.down[112:120] = jnp.zeros((8, D), F32)
+    swap1.take(0)
+    feed(0)
+    sum2.send_near(0)
+    turn(0)
+    sum2.relay(0)
+    gate_up_grads(0)
+    residual(1)
+    down_grads(0)
+    swap1.take(1)
+    sum1.drain()
+    feed(1)
     sum2.send_near(1)
-    gather1.forward()
-    gather1.all_ready()
-    feed(1 - own_pair)
-    sum2.send_near(0)
-    sum2.relay()
-
-    for q in range(4):
-        r.turned[:, 128 * q : 128 * q + 128] = r.nh[q].T
-
-    @pl.loop(0, 8)
-    def _(c):
-        rows = r.turned[rows_at(0, c, 160)]
-        z, x = lax.div(c, 2), 2 * lax.rem(c, 2)
-        for grad, row in ((r.gg, 0), (r.ug, 40)):
-            for job, lo, hi in ((GU1, 0, 256), (GU1, 256, 512), (GU1, 512, 640), (GU2, 640, 896)):
-                got = nn(rows, grad[:, lo:hi])
-                col = lo if job == GU1 else 0
-                for j in range(4):
-                    jobs[job].grad[z, x + j // 2, j % 2, row : row + 40, col : col + hi - lo] = got[
-                        40 * j : 40 * j + 40
-                    ].astype(BF16)
-
+    turn(1)
+    sum2.relay(1)
+    gate_up_grads(1)
     jobs[GU1].start1()
     jobs[GU2].start1()
-
-    for c in range(2):
-        sum2.arrive(c)
-
-        @pl.loop(0, 2)
-        def _(k):
-            at = rows_at(64 * c, k, 32)
-            res = r.res[at]
-            grad = r.cot[g, at].astype(F32) + norm_backward(res, inverse_rms(res), sum2.total(at) * fgain[...])
-            r.resg[at] = grad
-            r.rh[g, at] = grad.astype(BF16)
-
-        gather2.send(c)
-    sum2.drain()
-
-    for q in range(4):
-        r.turned[0:UNITS, 128 * q : 128 * q + 128] = r.hid[128 * q : 128 * q + 128].T
-    r.down[112:120] = jnp.zeros((8, D), F32)
-
-    @pl.loop(0, 8)
-    def _(c):
-        rows = r.turned[rows_at(0, c, 112)]
-        for lo, hi in WIDE_TILES:
-            r.down[0:112, lo:hi] = nn(rows, r.cot[:, :, lo:hi].reshape(512, hi - lo))
-        z, x = lax.div(c, 2), 2 * lax.rem(c, 2)
-        for j in range(4):
-            jobs[DN].grad[z, x + j // 2, j % 2] = r.down[28 * j : 28 * j + 32].astype(BF16)
-
+    residual_back(0)
+    down_grads(1)
     jobs[DN].start1()
 
     r.keyg[...] = jnp.zeros((128, 256), F32)
@@ -575,27 +640,30 @@
             r.valg[:, cols] += tn(prob.astype(BF16), agrad[:, cols])
             r.qgrad[qi, :, cols] = norm_backward(full, inverse, grad).astype(BF16)
 
-    attend_back(g)
-    gather2.chip_ready()
-    attend_back(mate)
-    gather2.forward()
+    attend_back(core)
+    swap2.take(0)
+    attend_back(1 - core)
+    residual_back(1)
     jobs[GU1].relay1()
     jobs[GU2].relay1()
-    attend_back(over)
-    gather2.all_ready()
-    attend_back(over_mate)
+    attend_back(2 + core)
+    swap2.take(1)
+    sum2.drain()
+    attend_back(3 - core)
     for h in range(2):
         cols = slice(HEAD * h, HEAD * h + HEAD)
         full = r.key[:, cols]
         r.kg[:, cols] = norm_backward(full, inverse_rms(full), r.keyg[:, cols]).astype(BF16)
     r.vg[...] = r.valg[...].astype(BF16)
 
-    @pl.loop(0, 32)
-    def _(p):
-        rows = r.patches[:, rows_at(0, p, 128)].T
-        at = (lax.div(p, 8), lax.rem(lax.div(p, 2), 4), lax.rem(p, 2))
-        jobs[KK].grad[at] = nn(rows, r.kg[...]).astype(BF16)
-        jobs[VV].grad[at] = nn(rows, r.vg[...]).astype(BF16)
+    @pl.loop(0, 8)
+    def _(n):
+        rows = r.patches[:, rows_at(0, n, 512)].T
+        z, x = lax.div(n, 2), 2 * lax.rem(n, 2)
+        for job, grad in ((KK, r.kg), (VV, r.vg)):
+            got = nn(rows, grad[...]).astype(BF16)
+            for j in range(4):
+                jobs[job].grad[z, x + j // 2, j % 2] = got[128 * j : 128 * j + 128]
 
     jobs[KK].start1()
     jobs[VV].start1()
@@ -656,7 +724,7 @@
         def _(k):
             at = rows_at(64 * c, k, 32)
             x = r.states[g, at].astype(F32)
-            grad = r.resg[at] + norm_backward(x, inverse_rms(x), sum3.total(at) * again[...])
+            grad = r.res[lax.div(g, 2), at] + norm_backward(x, inverse_rms(x), sum3.total(at) * r.gain1[...])
             out_bytes[at] = grad.astype(BF16)
 
     for c in range(2):
@@ -679,7 +747,7 @@
         jobs[n].start3()
     for n in (KK, VV, QO):
         place_piece(n, jobs[n].finish(), flat)
-    for item in (*jobs, sum3, sum4, gather1, gather2):
+    for item in (*jobs, sum3, sum4, swap1, swap2):
         item.drain()
 
 
@@ -719,8 +787,8 @@
         ),
     )(
         patch_lengths,
-        attention_gain.reshape(1, D),
-        feedforward_gain.reshape(1, D),
+        attention_gain,
+        feedforward_gain,
         byte_states.reshape(4, 128, D),
         patch_states,
         cotangent.reshape(4, 128, D),
@@ -732,6 +800,7 @@
         up_weight,
         down_weight,
     )
+    summed, adam_first, adam_second = lax.optimization_barrier((summed, adam_first, adam_second))
     gradient = summed * float(row_count * piece_count) ** (-0.5)
     new_first = beta_first * adam_first.reshape(FLAT, 128) + (1.0 - beta_first) * gradient
     new_second = beta_second * adam_second.reshape(FLAT, 128) + (1.0 - beta_second) * gradient * gradient

time: 131 us -> 126 us (0.962)
  local copies, waits for them, and re-layouts: 4.1 us -> 1.44 us
  other arithmetic: 6.42 us -> 4.3 us
    reshape x2 -> x0, local copies, waits for them, and re-layouts: 2.66 us -> none  [the longest x1 1.37 us: shards(): attention_gain.reshape(1, D)]
    mul x1 -> x0, other arithmetic: 1.82 us -> none  [shards(): beta_first * adam_first.reshape(FLAT, 128) + (1.0 - beta_first) * gradient]
    div x1, other arithmetic: 3.02 us -> 1.61 us  [shards(): new_first / bias_first / (jnp.sqrt(new_second / bias_second) + adam_epsilon)]
where the time goes in v3:
time: 126 us; the launch traced here: 125 us
  Pallas kernels  119 us (94%)
  other arithmetic  4.3 us (3%)
  local copies, waits for them, and re-layouts  1.44 us (1%)
    pallas_call x1, Pallas kernels, shards(): pl.pallas_call(layer_kernel, out_shape=(jax.ShapeDtypeStruct((FLAT, 128),...  119 us
    mul x1, other arithmetic, shards(): beta_second * adam_second.reshape(FLAT, 128)  2.69 us

profile of v3, /device:TPU:0, one launch (start us, length us, event | category | flops | bytes accessed | tf_op | source)
XLA Modules:
  0.0 125.1 jit_solution(12380323044702894848)
XLA Ops:
  0.6 0.0 copy-start
  0.6 118.7 %shard_map.182 = (f32[1512,128]{1,0:T(8,128)}, bf16[128,1280]{1,0:T(8,128)(2,1)}, bf16[32,4096]{1,0:T(8,128)(2,1)}) custom-call(s32[1,128]{1,0:T(1,128)} %refs_0_.1, f32[1280]{0:T(1024)} %refs_1_.1, f32[1280]{0:T(1024)} %refs_2_.1, bf16[4,128,1280]{2,1,0:T(8,128)(2,1)} %bitcast.9, bf16[128,4096]{1,0:T(8,128)(2,1)} %refs_4_.1, ...), custom_call_target="tpu_custom_call" | custom-call | tf_op jit(solution)/shard_map/pallas_call | solution.py:775
  119.3 0.0 copy-start.1
  119.3 0.0 copy-done
  119.3 2.7 %broadcast_multiply_fusion = (f32[1,193536]{1,0:T(1,128)S(1)}, f32[1,193536]{1,0:T(1,128)S(1)}) fusion(f32[1,193536]{1,0:T(1,128)S(1)} %copy-done, f32[1,193536]{1,0:T(1,128)} %param.28), kind=kLoop, calls=%fused_computation.3 | loop fusion | flops 387072 | bytes 3096576 | tf_op jit(solution)/shard_map/mul | solution.py:806
  122.0 0.0 copy-done.1
  122.0 0.0 copy-start.2
  122.0 0.0 copy-start.3
  122.1 1.6 %add_divide_fusion = (f32[1512,128]{1,0:T(8,128)}, f32[1512,128]{1,0:T(8,128)}, f32[1512,128]{1,0:T(8,128)}) fusion(f32[1512,128]{1,0:T(8,128)S(1)} %bitcast.7, f32[1512,128]{1,0:T(8,128)S(1)} %copy-done.1, f32[1512,128]{1,0:T(8,128)S(1)} %bitcast.8), kind=kLoop, calls=%fused_computation | loop fusion | flops 1935360 | bytes 4644864 | tf_op jit(solution)/shard_map/div | solution.py:807
  123.7 0.0 copy-done.2
  123.7 0.7 copy.22
  124.4 0.0 copy-done.3
  124.4 0.7 copy.23
Async XLA Ops:
  0.6 118.7 %copy-start = (f32[1,193536]{1,0:T(1,128)S(1)}, f32[1,193536]{1,0:T(1,128)}, u32[]{:S(2)}) copy-start(f32[1,193536]{1,0:T(1,128)} %param.29) | copy-start | bytes 2322436
  119.3 2.7 %copy-start.1 = (f32[1512,128]{1,0:T(8,128)S(1)}, f32[1512,128]{1,0:T(8,128)}, u32[]{:S(2)}) copy-start(f32[1512,128]{1,0:T(8,128)} %get-tuple-element.15) | copy-start | bytes 2322436
  122.0 1.6 %copy-start.2 = (bf16[128,1280]{1,0:T(8,128)(2,1)S(1)}, bf16[128,1280]{1,0:T(8,128)(2,1)}, u32[]{:S(2)}) copy-start(bf16[128,1280]{1,0:T(8,128)(2,1)} %get-tuple-element.27) | copy-start | bytes 983044
  122.0 2.4 %copy-start.3 = (bf16[32,4096]{1,0:T(8,128)(2,1)S(1)}, bf16[32,4096]{1,0:T(8,128)(2,1)}, u32[]{:S(2)}) copy-start(bf16[32,4096]{1,0:T(8,128)(2,1)} %get-tuple-element.28) | copy-start | bytes 786436

commit v4 on v3

--- a/solution.py
+++ b/solution.py
@@ -26,6 +26,7 @@
 UNIT_TILES = ((0, 256), (256, 512), (512, 768), (768, 896))
 WIDE_TILES = tuple((n, n + 256) for n in range(0, D, 256))
 FLAT = 1512
+TOKEN_SCALE = 16384.0**-0.5
 
 GU1, GU2, DN, KK, VV, QO = range(6)
 PIECES = (
@@ -80,9 +81,9 @@
         pltpu.VMEM((4, 4, 2, rows, cols), BF16),
         pltpu.VMEM((2, 2, 2, rows, cols), BF16),
         pltpu.VMEM((2, 4, 2, rows, cols), BF16),
+        pltpu.VMEM((4, rows, cols), BF16),
+        pltpu.VMEM((rows, cols), BF16),
         pltpu.VMEM((2, rows, cols), BF16),
-        pltpu.VMEM((2, 2, rows, cols), BF16),
-        pltpu.VMEM((rows, cols), BF16),
         pltpu.SemaphoreType.DMA((13,)),
         pltpu.SemaphoreType.DMA((13,)),
     ]
@@ -90,8 +91,10 @@
 
 class Scatter:
     def __init__(self, item, refs):
-        self.zfirst = PIECES[item][2]
-        self.grad, self.near, self.got, self.near2, self.got2, self.last, self.send, self.recv = refs
+        rows, _, self.zfirst = PIECES[item]
+        cut = 16 * ((rows // 16 + 1) // 2)
+        self.halves = (slice(0, cut), slice(cut, rows))
+        self.grad, self.near, self.got, self.pairs, self.near2, self.got2, self.send, self.recv = refs
         z, x, self.y, self.g = place()
         self.f, self.s = (z, x) if self.zfirst else (x, z)
         self.live = {}
@@ -136,47 +139,54 @@
 
             self.copy(4 + i, self.near.at[i], self.got.at[i, pl.ds(2 * i, 2)], dev)
 
-    def start2(self):
+    def sum_mine(self, y):
+        @pl.loop(0, 4)
+        def _(a):
+            own = self.grad[self.mine(a, y)].astype(F32)
+            total = own + self.got[0, a, y].astype(F32) + self.got[1, a, y].astype(F32)
+            self.grad[self.mine(a, y)] = total.astype(BF16)
+
+    def swap(self):
         for n in (2, 3, 4, 5):
             self.live[n].wait_recv()
-
-        @pl.loop(0, 8)
-        def _(k):
-            a, b = lax.div(k, 2), lax.rem(k, 2)
-            own = self.grad[self.mine(a, b)].astype(F32)
-            total = own + self.got[0, a, b].astype(F32) + self.got[1, a, b].astype(F32)
-            self.grad[self.mine(a, b)] = total.astype(BF16)
+        other = 1 - self.y
+        self.sum_mine(other)
+        self.copy(12, self.grad.at[self.mine(slice(None), other)], self.pairs, self.who(self.f, self.s, other))
+        self.sum_mine(self.y)
+
+    def start2(self):
+        self.live[12].wait_recv()
+
+        @pl.loop(0, 4)
+        def _(a):
+            at = self.mine(a, self.y)
+            self.grad[at] = (self.grad[at].astype(F32) + self.pairs[a].astype(F32)).astype(BF16)
 
         for i, d in enumerate((1, 3)):
             dev = self.who(self.f, lax.rem(self.s + d, 4), self.y)
-            self.copy(6 + i, self.grad.at[self.mine(lax.rem(self.s + 2, 4), i)], self.near2.at[i], dev)
+            at = self.halves[i]
+            self.copy(6 + i, self.grad.at[(*self.mine(lax.rem(self.s + 2, 4), self.y), at)], self.near2.at[at], dev)
         for i, d in enumerate((1, 3)):
             nxt = lax.rem(self.s + d, 4)
             dev = self.who(self.f, nxt, self.y)
-            self.copy(8 + i, self.grad.at[self.mine(nxt, 1 - i)], self.got2.at[i, 1 - i], dev)
+            at = self.halves[1 - i]
+            self.copy(8 + i, self.grad.at[(*self.mine(nxt, self.y), at)], self.got2.at[i, at], dev)
 
     def relay2(self):
         for i, d in enumerate((1, 3)):
             nxt = lax.rem(self.s + d, 4)
             dev = self.who(self.f, nxt, self.y)
+            at = self.halves[i]
             self.live[6 + i].wait_recv()
-            own = self.grad[self.mine(nxt, i)].astype(F32)
-            self.near2[i] = (own + self.near2[i].astype(F32)).astype(BF16)
-            self.copy(10 + i, self.near2.at[i], self.got2.at[i, i], dev)
-
-    def start3(self):
+            own = self.grad[(*self.mine(nxt, self.y), at)].astype(F32)
+            self.near2[at] = (own + self.near2[at].astype(F32)).astype(BF16)
+            self.copy(10 + i, self.near2.at[at], self.got2.at[i, at], dev)
+
+    def finish(self):
         for n in (8, 9, 10, 11):
             self.live[n].wait_recv()
-        for b in range(2):
-            own = self.grad[self.mine(self.s, b)].astype(F32)
-            total = own + self.got2[0, b].astype(F32) + self.got2[1, b].astype(F32)
-            self.grad[self.mine(self.s, b)] = total.astype(BF16)
-        other = 1 - self.y
-        self.copy(12, self.grad.at[self.mine(self.s, other)], self.last, self.who(self.f, self.s, other))
-
-    def finish(self):
-        self.live[12].wait_recv()
-        return self.grad[self.mine(self.s, self.y)].astype(F32) + self.last[...].astype(F32)
+        own = self.grad[self.mine(self.s, self.y)].astype(F32)
+        return own + self.got2[0].astype(F32) + self.got2[1].astype(F32)
 
     def drain(self):
         for c in self.live.values():
@@ -665,9 +675,10 @@
             for j in range(4):
                 jobs[job].grad[z, x + j // 2, j % 2] = got[128 * j : 128 * j + 128]
 
+    jobs[DN].relay1()
     jobs[KK].start1()
     jobs[VV].start1()
-    jobs[DN].relay1()
+    jobs[GU2].swap()
 
     for q in range(4):
         r.turned[:, 128 * q : 128 * q + 128] = r.normed[q].T
@@ -710,12 +721,16 @@
     sum4.send_near(1)
     sum3.relay()
     sum4.relay()
-    for n in (GU1, GU2, DN):
-        jobs[n].start2()
-    for n in (KK, VV, QO):
-        jobs[n].relay1()
-    for n in (GU1, GU2, DN):
-        jobs[n].relay2()
+    jobs[GU1].swap()
+    jobs[KK].relay1()
+    jobs[GU2].start2()
+    jobs[DN].swap()
+    jobs[VV].relay1()
+    jobs[GU2].relay2()
+    jobs[QO].relay1()
+    jobs[GU1].start2()
+    jobs[DN].start2()
+    jobs[GU1].relay2()
 
     for c in range(2):
         sum3.arrive(c)
@@ -735,20 +750,51 @@
             at = (pl.ds(16 * c, 16), rows_at(0, k, 1024))
             out_patches[at] = sum4.total(*at).astype(BF16)
 
-    for n in (KK, VV, QO):
-        jobs[n].start2()
-    for n in (GU1, GU2, DN):
-        jobs[n].start3()
-    for n in (KK, VV, QO):
+    jobs[DN].relay2()
+    place_piece(GU2, jobs[GU2].finish(), flat)
+    jobs[KK].swap()
+    jobs[VV].swap()
+    place_piece(GU1, jobs[GU1].finish(), flat)
+    place_piece(DN, jobs[DN].finish(), flat)
+    jobs[KK].start2()
+    jobs[QO].swap()
+    jobs[VV].start2()
+    for n in (KK, VV):
         jobs[n].relay2()
-    for n in (GU1, GU2, DN):
-        place_piece(n, jobs[n].finish(), flat)
-    for n in (KK, VV, QO):
-        jobs[n].start3()
+    jobs[QO].start2()
+    jobs[QO].relay2()
     for n in (KK, VV, QO):
         place_piece(n, jobs[n].finish(), flat)
     for item in (*jobs, sum3, sum4, swap1, swap2):
         item.drain()
+
+
+def adam_kernel(summed, first, second, bytes_in, patches_in, new_first, new_second, step, bytes_out, patches_out):
+    @pl.when(pl.program_id(0) == 0)
+    def _():
+        bytes_out[...] = bytes_in[...]
+        patches_out[...] = patches_in[...]
+
+    gradient = summed[...] * TOKEN_SCALE
+    moment = beta_first * first[...] + (1.0 - beta_first) * gradient
+    spread = beta_second * second[...] + (1.0 - beta_second) * gradient * gradient
+    new_first[...] = moment
+    new_second[...] = spread
+    step[...] = moment / bias_first / (jnp.sqrt(spread / bias_second) + adam_epsilon)
+
+
+def adam(summed, first, second, input_grad, patch_grad):
+    flat = pl.BlockSpec((216, 128), lambda i: (i, 0))
+    whole = [pl.BlockSpec(m.shape, lambda i: (0, 0)) for m in (input_grad, patch_grad)]
+    return pl.pallas_call(
+        adam_kernel,
+        grid=(7,),
+        out_shape=[jax.ShapeDtypeStruct((FLAT, 128), F32)] * 3
+        + [jax.ShapeDtypeStruct(m.shape, m.dtype) for m in (input_grad, patch_grad)],
+        in_specs=[flat] * 3 + whole,
+        out_specs=[flat] * 3 + whole,
+        compiler_params=pltpu.CompilerParams(vmem_limit_bytes=60 * MIB),
+    )(summed, first, second, input_grad, patch_grad)
 
 
 def shards(
@@ -768,8 +814,6 @@
     adam_first,
     adam_second,
 ):
-    row_count = byte_states.shape[0]
-    piece_count = lax.axis_size("dp")
     plain, sums, jobs = layer_scratch()
     vmem = pl.BlockSpec(memory_space=pltpu.VMEM)
     summed, input_grad, patch_grad = pl.pallas_call(
@@ -800,11 +844,9 @@
         up_weight,
         down_weight,
     )
-    summed, adam_first, adam_second = lax.optimization_barrier((summed, adam_first, adam_second))
-    gradient = summed * float(row_count * piece_count) ** (-0.5)
-    new_first = beta_first * adam_first.reshape(FLAT, 128) + (1.0 - beta_first) * gradient
-    new_second = beta_second * adam_second.reshape(FLAT, 128) + (1.0 - beta_second) * gradient * gradient
-    adam_step = new_first / bias_first / (jnp.sqrt(new_second / bias_second) + adam_epsilon)
+    new_first, new_second, adam_step, input_grad, patch_grad = adam(
+        summed, adam_first.reshape(FLAT, 128), adam_second.reshape(FLAT, 128), input_grad, patch_grad
+    )
     return (
         input_grad,
         patch_grad,

time: 126 us -> 142 us (1.13)
  Pallas kernels: 119 us -> 141 us
  other arithmetic: 4.3 us -> 0 us
  local copies, waits for them, and re-layouts: 1.44 us -> 0 us
    pallas_call x1, Pallas kernels: 119 us -> 135 us  [shards(): pl.pallas_call(layer_kernel, out_shape=(jax.ShapeDtypeStruct((FLAT, 128),...]
    pallas_call x0 -> x1, Pallas kernels: none -> 5.98 us  [adam(): pl.pallas_call(adam_kernel, grid=(7,), out_shape=[jax.ShapeDtypeStruct((F...]
    mul x1 -> x0, other arithmetic: 2.69 us -> none  [shards(): beta_second * adam_second.reshape(FLAT, 128)]
    div x1 -> x0, other arithmetic: 1.61 us -> none  [shards(): new_first / bias_first / (jnp.sqrt(new_second / bias_second) + adam_epsilon)]
    unnamed x10 -> x0, local copies, waits for them, and re-layouts: 1.44 us -> none
where the time goes in v4:
time: 142 us
  Pallas kernels  141 us (99%)
    pallas_call x1, Pallas kernels, shards(): pl.pallas_call(layer_kernel, out_shape=(jax.ShapeDtypeStruct((FLAT, 128),...  135 us
    pallas_call x1, Pallas kernels, adam(): pl.pallas_call(adam_kernel, grid=(7,), out_shape=[jax.ShapeDtypeStruct((F...  5.98 us

profile of v4, /device:TPU:0, one launch (start us, length us, event | category | flops | bytes accessed | tf_op | source)
XLA Modules:
  0.0 141.8 jit_solution(8463616900625267799)
XLA Ops:
  0.6 135.0 %shard_map.182 = (f32[1512,128]{1,0:T(8,128)}, bf16[128,1280]{1,0:T(8,128)(2,1)}, bf16[32,4096]{1,0:T(8,128)(2,1)}) custom-call(s32[1,128]{1,0:T(1,128)} %refs_0_.1, f32[1280]{0:T(1024)} %refs_1_.1, f32[1280]{0:T(1024)} %refs_2_.1, bf16[4,128,1280]{2,1,0:T(8,128)(2,1)} %bitcast.7, bf16[128,4096]{1,0:T(8,128)(2,1)} %refs_4_.1, bf16[4,128,1280]{2,1,0:T(8,128)(2,1)} %bitcast.8, ...), custom_call_target="tpu_custom_call" | custom-call | tf_op jit(solution)/shard_map/pallas_call | solution.py:819
  135.7 6.0 %shard_map.183 = (f32[1512,128]{1,0:T(8,128)}, f32[1512,128]{1,0:T(8,128)}, f32[1512,128]{1,0:T(8,128)}, bf16[128,1280]{1,0:T(8,128)(2,1)}, bf16[32,4096]{1,0:T(8,128)(2,1)}) custom-call(f32[1512,128]{1,0:T(8,128)} %get-tuple-element.13.summed, f32[1512,128]{1,0:T(8,128)} %bitcast.9, f32[1512,128]{1,0:T(8,128)} %bitcast.10, ...), custom_call_target="tpu_custom_call" | custom-call | tf_op jit(solution)/shard_map/pallas_call | solution.py:789

commit v5 on v3

--- a/solution.py
+++ b/solution.py
@@ -26,6 +26,7 @@
 UNIT_TILES = ((0, 256), (256, 512), (512, 768), (768, 896))
 WIDE_TILES = tuple((n, n + 256) for n in range(0, D, 256))
 FLAT = 1512
+TOKEN_SCALE = 16384.0**-0.5
 
 GU1, GU2, DN, KK, VV, QO = range(6)
 PIECES = (
@@ -36,6 +37,7 @@
     (128, 256, False),
     (160, 128, True),
 )
+LATE = (KK, VV, QO)
 
 
 def nn(left, right):
@@ -76,13 +78,13 @@
 
 def scatter_scratch(item):
     rows, cols, _ = PIECES[item]
+    shapes = ((2,), (2, 2), ()) if item in LATE else ((4,), (), (2,))
+    ends = [pltpu.VMEM((*m, rows, cols), BF16) for m in shapes]
     return [
         pltpu.VMEM((4, 4, 2, rows, cols), BF16),
         pltpu.VMEM((2, 2, 2, rows, cols), BF16),
         pltpu.VMEM((2, 4, 2, rows, cols), BF16),
-        pltpu.VMEM((2, rows, cols), BF16),
-        pltpu.VMEM((2, 2, rows, cols), BF16),
-        pltpu.VMEM((rows, cols), BF16),
+        *ends,
         pltpu.SemaphoreType.DMA((13,)),
         pltpu.SemaphoreType.DMA((13,)),
     ]
@@ -90,11 +92,16 @@
 
 class Scatter:
     def __init__(self, item, refs):
-        self.zfirst = PIECES[item][2]
-        self.grad, self.near, self.got, self.near2, self.got2, self.last, self.send, self.recv = refs
+        rows, _, self.zfirst = PIECES[item]
+        cut = 16 * ((rows // 16 + 1) // 2)
+        self.halves = (slice(0, cut), slice(cut, rows))
+        self.unpack(refs)
         z, x, self.y, self.g = place()
         self.f, self.s = (z, x) if self.zfirst else (x, z)
         self.live = {}
+
+    def unpack(self, refs):
+        self.grad, self.near, self.got, self.pairs, self.near2, self.got2, self.send, self.recv = refs
 
     def at(self, f, s):
         return (f, s) if self.zfirst else (s, f)
@@ -136,6 +143,64 @@
 
             self.copy(4 + i, self.near.at[i], self.got.at[i, pl.ds(2 * i, 2)], dev)
 
+    def sum_mine(self, y):
+        @pl.loop(0, 4)
+        def _(a):
+            own = self.grad[self.mine(a, y)].astype(F32)
+            total = own + self.got[0, a, y].astype(F32) + self.got[1, a, y].astype(F32)
+            self.grad[self.mine(a, y)] = total.astype(BF16)
+
+    def swap(self):
+        for n in (2, 3, 4, 5):
+            self.live[n].wait_recv()
+        other = 1 - self.y
+        self.sum_mine(other)
+        self.copy(12, self.grad.at[self.mine(slice(None), other)], self.pairs, self.who(self.f, self.s, other))
+        self.sum_mine(self.y)
+
+    def start2(self):
+        self.live[12].wait_recv()
+
+        @pl.loop(0, 4)
+        def _(a):
+            at = self.mine(a, self.y)
+            self.grad[at] = (self.grad[at].astype(F32) + self.pairs[a].astype(F32)).astype(BF16)
+
+        for i, d in enumerate((1, 3)):
+            dev = self.who(self.f, lax.rem(self.s + d, 4), self.y)
+            at = self.halves[i]
+            self.copy(6 + i, self.grad.at[(*self.mine(lax.rem(self.s + 2, 4), self.y), at)], self.near2.at[at], dev)
+        for i, d in enumerate((1, 3)):
+            nxt = lax.rem(self.s + d, 4)
+            dev = self.who(self.f, nxt, self.y)
+            at = self.halves[1 - i]
+            self.copy(8 + i, self.grad.at[(*self.mine(nxt, self.y), at)], self.got2.at[i, at], dev)
+
+    def relay2(self):
+        for i, d in enumerate((1, 3)):
+            nxt = lax.rem(self.s + d, 4)
+            dev = self.who(self.f, nxt, self.y)
+            at = self.halves[i]
+            self.live[6 + i].wait_recv()
+            own = self.grad[(*self.mine(nxt, self.y), at)].astype(F32)
+            self.near2[at] = (own + self.near2[at].astype(F32)).astype(BF16)
+            self.copy(10 + i, self.near2.at[at], self.got2.at[i, at], dev)
+
+    def finish(self):
+        for n in (8, 9, 10, 11):
+            self.live[n].wait_recv()
+        own = self.grad[self.mine(self.s, self.y)].astype(F32)
+        return own + self.got2[0].astype(F32) + self.got2[1].astype(F32)
+
+    def drain(self):
+        for c in self.live.values():
+            c.wait_send()
+
+
+class ScatterLate(Scatter):
+    def unpack(self, refs):
+        self.grad, self.near, self.got, self.near2, self.got2, self.last, self.send, self.recv = refs
+
     def start2(self):
         for n in (2, 3, 4, 5):
             self.live[n].wait_recv()
@@ -177,10 +242,6 @@
     def finish(self):
         self.live[12].wait_recv()
         return self.grad[self.mine(self.s, self.y)].astype(F32) + self.last[...].astype(F32)
-
-    def drain(self):
-        for c in self.live.values():
-            c.wait_send()
 
 
 def heads_place():
@@ -429,7 +490,7 @@
     r.hid = r.wd.at[0:512, 0:UNITS]
     r.attt = r.wd.at[512:768, 0:512]
     sum_refs = [[rest.pop(0) for _ in s] for s in sums]
-    jobs = [Scatter(i, [rest.pop(0) for _ in s]) for i, s in enumerate(jobs)]
+    jobs = [(ScatterLate if i in LATE else Scatter)(i, [rest.pop(0) for _ in s]) for i, s in enumerate(jobs)]
     g, _, _, _ = heads_place()
     core = lax.rem(g, 2)
 
@@ -622,6 +683,7 @@
     jobs[GU2].start1()
     residual_back(0)
     down_grads(1)
+    jobs[GU2].relay1()
     jobs[DN].start1()
 
     r.keyg[...] = jnp.zeros((128, 256), F32)
@@ -644,8 +706,6 @@
     swap2.take(0)
     attend_back(1 - core)
     residual_back(1)
-    jobs[GU1].relay1()
-    jobs[GU2].relay1()
     attend_back(2 + core)
     swap2.take(1)
     sum2.drain()
@@ -656,6 +716,8 @@
         r.kg[:, cols] = norm_backward(full, inverse_rms(full), r.keyg[:, cols]).astype(BF16)
     r.vg[...] = r.valg[...].astype(BF16)
 
+    jobs[GU1].relay1()
+
     @pl.loop(0, 8)
     def _(n):
         rows = r.patches[:, rows_at(0, n, 512)].T
@@ -665,9 +727,8 @@
             for j in range(4):
                 jobs[job].grad[z, x + j // 2, j % 2] = got[128 * j : 128 * j + 128]
 
+    jobs[VV].start1()
     jobs[KK].start1()
-    jobs[VV].start1()
-    jobs[DN].relay1()
 
     for q in range(4):
         r.turned[:, 128 * q : 128 * q + 128] = r.normed[q].T
@@ -689,7 +750,6 @@
             blocks += [m[:, 128 * n : 128 * n + 128] for m in halves for n in range(5)]
             jobs[QO].grad[c, j // 2, j % 2] = jnp.concatenate(blocks, axis=0).astype(BF16)
 
-    jobs[QO].start1()
 
     @pl.loop(0, 2)
     def _(p):
@@ -709,13 +769,12 @@
     sum4.send_near(0)
     sum4.send_near(1)
     sum3.relay()
+    jobs[GU1].swap()
+    jobs[GU2].swap()
     sum4.relay()
-    for n in (GU1, GU2, DN):
-        jobs[n].start2()
-    for n in (KK, VV, QO):
-        jobs[n].relay1()
-    for n in (GU1, GU2, DN):
-        jobs[n].relay2()
+    jobs[DN].relay1()
+    jobs[KK].relay1()
+    jobs[VV].relay1()
 
     for c in range(2):
         sum3.arrive(c)
@@ -727,6 +786,11 @@
             grad = r.res[lax.div(g, 2), at] + norm_backward(x, inverse_rms(x), sum3.total(at) * r.gain1[...])
             out_bytes[at] = grad.astype(BF16)
 
+    jobs[QO].start1()
+    jobs[GU1].start2()
+    jobs[DN].swap()
+    jobs[QO].relay1()
+
     for c in range(2):
         sum4.arrive(c)
 
@@ -735,17 +799,21 @@
             at = (pl.ds(16 * c, 16), rows_at(0, k, 1024))
             out_patches[at] = sum4.total(*at).astype(BF16)
 
-    for n in (KK, VV, QO):
-        jobs[n].start2()
-    for n in (GU1, GU2, DN):
-        jobs[n].start3()
-    for n in (KK, VV, QO):
-        jobs[n].relay2()
-    for n in (GU1, GU2, DN):
-        place_piece(n, jobs[n].finish(), flat)
-    for n in (KK, VV, QO):
-        jobs[n].start3()
-    for n in (KK, VV, QO):
+    jobs[VV].start2()
+    jobs[KK].start2()
+    jobs[GU2].start2()
+    jobs[KK].relay2()
+    jobs[QO].start2()
+    jobs[VV].relay2()
+    jobs[GU1].relay2()
+    jobs[QO].relay2()
+    jobs[KK].start3()
+    jobs[DN].start2()
+    jobs[VV].start3()
+    jobs[GU2].relay2()
+    jobs[DN].relay2()
+    jobs[QO].start3()
+    for n in (GU1, GU2, KK, VV, DN, QO):
         place_piece(n, jobs[n].finish(), flat)
     for item in (*jobs, sum3, sum4, swap1, swap2):
         item.drain()
@@ -768,8 +836,6 @@
     adam_first,
     adam_second,
 ):
-    row_count = byte_states.shape[0]
-    piece_count = lax.axis_size("dp")
     plain, sums, jobs = layer_scratch()
     vmem = pl.BlockSpec(memory_space=pltpu.VMEM)
     summed, input_grad, patch_grad = pl.pallas_call(
@@ -801,7 +867,7 @@
         down_weight,
     )
     summed, adam_first, adam_second = lax.optimization_barrier((summed, adam_first, adam_second))
-    gradient = summed * float(row_count * piece_count) ** (-0.5)
+    gradient = summed * TOKEN_SCALE
     new_first = beta_first * adam_first.reshape(FLAT, 128) + (1.0 - beta_first) * gradient
     new_second = beta_second * adam_second.reshape(FLAT, 128) + (1.0 - beta_second) * gradient * gradient
     adam_step = new_first / bias_first / (jnp.sqrt(new_second / bias_second) + adam_epsilon)

time: 126 us -> 119 us (0.944)
  Pallas kernels: 119 us -> 112 us
    pallas_call x1, Pallas kernels: 119 us -> 112 us  [shards(): pl.pallas_call(layer_kernel, out_shape=(jax.ShapeDtypeStruct((FLAT, 128),...]
where the time goes in v5:
time: 119 us; the launch traced here: 118 us
  Pallas kernels  112 us (94%)
  other arithmetic  4.3 us (4%)
  local copies, waits for them, and re-layouts  1.44 us (1%)
    pallas_call x1, Pallas kernels, shards(): pl.pallas_call(layer_kernel, out_shape=(jax.ShapeDtypeStruct((FLAT, 128),...  112 us
    mul x1, other arithmetic, shards(): beta_second * adam_second.reshape(FLAT, 128)  2.69 us

profile of v5, /device:TPU:0, one launch (start us, length us, event | category | flops | bytes accessed | tf_op | source)
XLA Modules:
  0.0 118.2 jit_solution(1302427948336589592)
XLA Ops:
  0.6 0.0 copy-start
  0.6 111.8 %shard_map.182 = (f32[1512,128]{1,0:T(8,128)}, bf16[128,1280]{1,0:T(8,128)(2,1)}, bf16[32,4096]{1,0:T(8,128)(2,1)}) custom-call(s32[1,128]{1,0:T(1,128)} %refs_0_.1, f32[1280]{0:T(1024)} %refs_1_.1, f32[1280]{0:T(1024)} %refs_2_.1, bf16[4,128,1280]{2,1,0:T(8,128)(2,1)} %bitcast.9, bf16[128,4096]{1,0:T(8,128)(2,1)} %refs_4_.1, ...), custom_call_target="tpu_custom_call" | custom-call | tf_op jit(solution)/shard_map/pallas_call | solution.py:841
  112.4 0.0 copy-start.1
  112.4 0.0 copy-done
  112.5 2.7 %broadcast_multiply_fusion = (f32[1,193536]{1,0:T(1,128)S(1)}, f32[1,193536]{1,0:T(1,128)S(1)}) fusion(f32[1,193536]{1,0:T(1,128)S(1)} %copy-done, f32[1,193536]{1,0:T(1,128)} %param.28), kind=kLoop, calls=%fused_computation.3 | loop fusion | flops 387072 | bytes 3096576 | tf_op jit(solution)/shard_map/mul | solution.py:872
  115.2 0.0 copy-done.1
  115.2 0.0 copy-start.2
  115.2 0.0 copy-start.3
  115.2 1.6 %add_divide_fusion = (f32[1512,128]{1,0:T(8,128)}, f32[1512,128]{1,0:T(8,128)}, f32[1512,128]{1,0:T(8,128)}) fusion(f32[1512,128]{1,0:T(8,128)S(1)} %bitcast.7, f32[1512,128]{1,0:T(8,128)S(1)} %copy-done.1, f32[1512,128]{1,0:T(8,128)S(1)} %bitcast.8), kind=kLoop, calls=%fused_computation | loop fusion | flops 1935360 | bytes 4644864 | tf_op jit(solution)/shard_map/div | solution.py:873
  116.8 0.0 copy-done.2
  116.8 0.7 copy.22
  117.5 0.0 copy-done.3
  117.5 0.7 copy.23
Async XLA Ops:
  0.6 111.8 %copy-start = (f32[1,193536]{1,0:T(1,128)S(1)}, f32[1,193536]{1,0:T(1,128)}, u32[]{:S(2)}) copy-start(f32[1,193536]{1,0:T(1,128)} %param.29) | copy-start | bytes 2322436
  112.4 2.7 %copy-start.1 = (f32[1512,128]{1,0:T(8,128)S(1)}, f32[1512,128]{1,0:T(8,128)}, u32[]{:S(2)}) copy-start(f32[1512,128]{1,0:T(8,128)} %get-tuple-element.15) | copy-start | bytes 2322436
  115.2 1.6 %copy-start.2 = (bf16[128,1280]{1,0:T(8,128)(2,1)S(1)}, bf16[128,1280]{1,0:T(8,128)(2,1)}, u32[]{:S(2)}) copy-start(bf16[128,1280]{1,0:T(8,128)(2,1)} %get-tuple-element.27) | copy-start | bytes 983044
  115.2 2.4 %copy-start.3 = (bf16[32,4096]{1,0:T(8,128)(2,1)S(1)}, bf16[32,4096]{1,0:T(8,128)(2,1)}, u32[]{:S(2)}) copy-start(bf16[32,4096]{1,0:T(8,128)(2,1)} %get-tuple-element.28) | copy-start | bytes 786436

commit v6 on v5

--- a/solution.py
+++ b/solution.py
@@ -817,6 +817,30 @@
         place_piece(n, jobs[n].finish(), flat)
     for item in (*jobs, sum3, sum4, swap1, swap2):
         item.drain()
+
+
+def adam_kernel(summed, first, second, bytes_in, patches_in, new_first, new_second, step, bytes_out, patches_out):
+    bytes_out[...] = bytes_in[...]
+    patches_out[...] = patches_in[...]
+
+    gradient = summed[...] * TOKEN_SCALE
+    moment = beta_first * first[...] + (1.0 - beta_first) * gradient
+    spread = beta_second * second[...] + (1.0 - beta_second) * gradient * gradient
+    new_first[...] = moment
+    new_second[...] = spread
+    step[...] = moment / bias_first / (jnp.sqrt(spread / bias_second) + adam_epsilon)
+
+
+def adam(summed, first, second, input_grad, patch_grad):
+    vmem = pl.BlockSpec(memory_space=pltpu.VMEM)
+    return pl.pallas_call(
+        adam_kernel,
+        out_shape=[jax.ShapeDtypeStruct((FLAT, 128), F32)] * 3
+        + [jax.ShapeDtypeStruct(m.shape, m.dtype) for m in (input_grad, patch_grad)],
+        in_specs=[vmem] * 5,
+        out_specs=[vmem] * 5,
+        compiler_params=pltpu.CompilerParams(vmem_limit_bytes=60 * MIB),
+    )(summed, first, second, input_grad, patch_grad)
 
 
 def shards(
@@ -866,11 +890,9 @@
         up_weight,
         down_weight,
     )
-    summed, adam_first, adam_second = lax.optimization_barrier((summed, adam_first, adam_second))
-    gradient = summed * TOKEN_SCALE
-    new_first = beta_first * adam_first.reshape(FLAT, 128) + (1.0 - beta_first) * gradient
-    new_second = beta_second * adam_second.reshape(FLAT, 128) + (1.0 - beta_second) * gradient * gradient
-    adam_step = new_first / bias_first / (jnp.sqrt(new_second / bias_second) + adam_epsilon)
+    new_first, new_second, adam_step, input_grad, patch_grad = adam(
+        summed, adam_first.reshape(FLAT, 128), adam_second.reshape(FLAT, 128), input_grad, patch_grad
+    )
     return (
         input_grad,
         patch_grad,

time: 119 us -> 116 us (0.975)
  other arithmetic: 4.3 us -> 0 us
  Pallas kernels: 112 us -> 115 us
  local copies, waits for them, and re-layouts: 1.44 us -> 0 us
    pallas_call x0 -> x1, Pallas kernels: none -> 3.6 us  [adam(): pl.pallas_call(adam_kernel, out_shape=[jax.ShapeDtypeStruct((FLAT, 128),...]
    mul x1 -> x0, other arithmetic: 2.69 us -> none  [shards(): beta_second * adam_second.reshape(FLAT, 128)]
    div x1 -> x0, other arithmetic: 1.61 us -> none  [shards(): new_first / bias_first / (jnp.sqrt(new_second / bias_second) + adam_epsilon)]
    unnamed x10 -> x0, local copies, waits for them, and re-layouts: 1.44 us -> none
where the time goes in v6:
time: 116 us
  Pallas kernels  115 us (99%)
    pallas_call x1, Pallas kernels, shards(): pl.pallas_call(layer_kernel, out_shape=(jax.ShapeDtypeStruct((FLAT, 128),...  112 us
    pallas_call x1, Pallas kernels, adam(): pl.pallas_call(adam_kernel, out_shape=[jax.ShapeDtypeStruct((FLAT, 128),...  3.6 us

profile of v6, /device:TPU:0, one launch (start us, length us, event | category | flops | bytes accessed | tf_op | source)
XLA Modules:
  0.0 115.9 jit_solution(7160354956947077750)
XLA Ops:
  0.6 111.7 %shard_map.182 = (f32[1512,128]{1,0:T(8,128)}, bf16[128,1280]{1,0:T(8,128)(2,1)}, bf16[32,4096]{1,0:T(8,128)(2,1)}) custom-call(s32[1,128]{1,0:T(1,128)} %refs_0_.1, f32[1280]{0:T(1024)} %refs_1_.1, f32[1280]{0:T(1024)} %refs_2_.1, bf16[4,128,1280]{2,1,0:T(8,128)(2,1)} %bitcast.7, bf16[128,4096]{1,0:T(8,128)(2,1)} %refs_4_.1, bf16[4,128,1280]{2,1,0:T(8,128)(2,1)} %bitcast.8, ...), custom_call_target="tpu_custom_call" | custom-call | tf_op jit(solution)/shard_map/pallas_call | solution.py:865
  112.3 3.6 %shard_map.183 = (f32[1512,128]{1,0:T(8,128)}, f32[1512,128]{1,0:T(8,128)}, f32[1512,128]{1,0:T(8,128)}, bf16[128,1280]{1,0:T(8,128)(2,1)}, bf16[32,4096]{1,0:T(8,128)(2,1)}) custom-call(f32[1512,128]{1,0:T(8,128)} %get-tuple-element.13.summed, f32[1512,128]{1,0:T(8,128)} %bitcast.9, f32[1512,128]{1,0:T(8,128)} %bitcast.10, ...), custom_call_target="tpu_custom_call" | custom-call | tf_op jit(solution)/shard_map/pallas_call | solution.py:836

commit v7 on v6

--- a/solution.py
+++ b/solution.py
@@ -119,10 +119,16 @@
         self.live[n] = c
 
     def start1(self):
+        self.start_far()
+        self.start_next()
+
+    def start_far(self):
         far = lax.rem(self.f + 2, 4)
         for i, d in enumerate((1, 3)):
             dev = self.who(lax.rem(self.f + d, 4), self.s, self.y)
             self.copy(i, self.grad.at[self.at(far, pl.ds(2 * i, 2))], self.near.at[i], dev)
+
+    def start_next(self):
         for i, d in enumerate((1, 3)):
             nxt = lax.rem(self.f + d, 4)
             dev = self.who(nxt, self.s, self.y)
@@ -420,7 +426,7 @@
     barrier = pltpu.get_barrier_semaphore()
     for dev in partners:
         pl.semaphore_signal(barrier, inc=1, device_id=dev, device_id_type=MESH_ID)
-    pl.semaphore_wait(barrier, len(partners))
+    return lambda: pl.semaphore_wait(barrier, len(partners))
 
 
 def rows_at(first, k, size):
@@ -505,7 +511,7 @@
         moves[name].start()
     r.gain1[...] = again[...].reshape(1, D)
     r.gain2[...] = fgain[...].reshape(1, D)
-    greet()
+    all_here = greet()
 
     sum1 = PairSum(r.part1, sum_refs[0])
     sum2 = PairSum(r.part2, sum_refs[1])
@@ -561,6 +567,8 @@
 
     for b in range(2):
         attend(2 * b + 1 - core)
+        if b == 0:
+            all_here()
         sum1.send_near(b)
         attend(2 * b + core)
         sum1.relay(b)
@@ -633,9 +641,10 @@
         for q in (2 * p, 2 * p + 1):
             r.turned[:, 128 * q : 128 * q + 128] = r.nh[q].T
 
-    def gate_up_grads(p):
-        @pl.loop(0, 8)
-        def _(c):
+    def gate_up_grads(p, count, chunk):
+        @pl.loop(0, count)
+        def _(k):
+            c = chunk(k)
             rows = r.turned[rows_at(0, c, 160), 256 * p : 256 * p + 256]
             z, x = lax.div(c, 2), 2 * lax.rem(c, 2)
             for grad, row in ((r.gg, 0), (r.ug, 40)):
@@ -669,7 +678,7 @@
     sum2.send_near(0)
     turn(0)
     sum2.relay(0)
-    gate_up_grads(0)
+    gate_up_grads(0, 8, lambda k: k)
     residual(1)
     down_grads(0)
     swap1.take(1)
@@ -678,14 +687,15 @@
     sum2.send_near(1)
     turn(1)
     sum2.relay(1)
-    gate_up_grads(1)
-    jobs[GU1].start1()
+    own_z = place()[0]
+    gate_up_grads(1, 2, lambda k: 2 * lax.rem(own_z + 2, 4) + k)
+    jobs[GU1].start_far()
+    gate_up_grads(1, 4, lambda k: 2 * lax.rem(own_z + 1 + 2 * lax.div(k, 2), 4) + lax.rem(k, 2))
+    jobs[GU1].start_next()
+    gate_up_grads(1, 2, lambda k: 2 * own_z + k)
     jobs[GU2].start1()
     residual_back(0)
     down_grads(1)
-    jobs[GU2].relay1()
-    jobs[DN].start1()
-
     r.keyg[...] = jnp.zeros((128, 256), F32)
     r.valg[...] = jnp.zeros((128, 256), F32)
 
@@ -705,6 +715,8 @@
     attend_back(core)
     swap2.take(0)
     attend_back(1 - core)
+    jobs[GU2].relay1()
+    jobs[DN].start1()
     residual_back(1)
     attend_back(2 + core)
     swap2.take(1)
@@ -729,6 +741,7 @@
 
     jobs[VV].start1()
     jobs[KK].start1()
+    jobs[GU2].swap()
 
     for q in range(4):
         r.turned[:, 128 * q : 128 * q + 128] = r.normed[q].T
@@ -770,7 +783,6 @@
     sum4.send_near(1)
     sum3.relay()
     jobs[GU1].swap()
-    jobs[GU2].swap()
     sum4.relay()
     jobs[DN].relay1()
     jobs[KK].relay1()

time: 116 us -> 116 us (level)
  no operation moved by 1% of the time
where the time goes in v7:
time: 116 us; the launch traced here: 115 us
  Pallas kernels  114 us (98%)
    pallas_call x1, Pallas kernels, shards(): pl.pallas_call(layer_kernel, out_shape=(jax.ShapeDtypeStruct((FLAT, 128),...  111 us
    pallas_call x1, Pallas kernels, adam(): pl.pallas_call(adam_kernel, out_shape=[jax.ShapeDtypeStruct((FLAT, 128),...  3.6 us

profile of v7, /device:TPU:0, one launch (start us, length us, event | category | flops | bytes accessed | tf_op | source)
XLA Modules:
  0.0 115.1 jit_solution(4578504775113242361)
XLA Ops:
  0.6 110.8 %shard_map.182 = (f32[1512,128]{1,0:T(8,128)}, bf16[128,1280]{1,0:T(8,128)(2,1)}, bf16[32,4096]{1,0:T(8,128)(2,1)}) custom-call(s32[1,128]{1,0:T(1,128)} %refs_0_.1, f32[1280]{0:T(1024)} %refs_1_.1, f32[1280]{0:T(1024)} %refs_2_.1, bf16[4,128,1280]{2,1,0:T(8,128)(2,1)} %bitcast.7, bf16[128,4096]{1,0:T(8,128)(2,1)} %refs_4_.1, bf16[4,128,1280]{2,1,0:T(8,128)(2,1)} %bitcast.8, ...), custom_call_target="tpu_custom_call" | custom-call | tf_op jit(solution)/shard_map/pallas_call | solution.py:877
  111.5 3.6 %shard_map.183 = (f32[1512,128]{1,0:T(8,128)}, f32[1512,128]{1,0:T(8,128)}, f32[1512,128]{1,0:T(8,128)}, bf16[128,1280]{1,0:T(8,128)(2,1)}, bf16[32,4096]{1,0:T(8,128)(2,1)}) custom-call(f32[1512,128]{1,0:T(8,128)} %get-tuple-element.13.summed, f32[1512,128]{1,0:T(8,128)} %bitcast.9, f32[1512,128]{1,0:T(8,128)} %bitcast.10, ...), custom_call_target="tpu_custom_call" | custom-call | tf_op jit(solution)/shard_map/pallas_call | solution.py:848

commit v8 on v7

--- a/solution.py
+++ b/solution.py
@@ -30,9 +30,9 @@
 
 GU1, GU2, DN, KK, VV, QO = range(6)
 PIECES = (
-    (80, 640, True),
-    (80, 256, False),
-    (32, 1280, False),
+    (80, 512, True),
+    (80, 384, False),
+    (32, 1152, False),
     (128, 256, True),
     (128, 256, False),
     (160, 128, True),
@@ -404,8 +404,10 @@
         spread_rows(flat, 336, 2, total)
     elif item == DN:
         spread_rows(flat, 1232, 10, total[0:28])
+        for m in range(7):
+            spread_rows(flat, 1241 + 40 * m, 10, total[28:32, 128 * m : 128 * m + 128])
     else:
-        first = 0 if item == GU1 else 5
+        first = 0 if item == GU1 else 4
         spread_rows(flat, 672 + first, 7, total[0:40])
         spread_rows(flat, 952 + first, 7, total[40:80])
 
@@ -470,7 +472,8 @@
         valg=pltpu.VMEM((128, 256), F32),
         kg=pltpu.VMEM((128, 256), BF16),
         vg=pltpu.VMEM((128, 256), BF16),
-        down=pltpu.VMEM((120, D), F32),
+        down=pltpu.VMEM((112, D), F32),
+        lined=pltpu.VMEM((32, 1152), F32),
         g1s=pltpu.SemaphoreType.DMA((4,)),
         g1r=pltpu.SemaphoreType.DMA((4,)),
         g2s=pltpu.SemaphoreType.DMA((4,)),
@@ -648,9 +651,9 @@
             rows = r.turned[rows_at(0, c, 160), 256 * p : 256 * p + 256]
             z, x = lax.div(c, 2), 2 * lax.rem(c, 2)
             for grad, row in ((r.gg, 0), (r.ug, 40)):
-                for job, lo, hi in ((GU1, 0, 256), (GU1, 256, 512), (GU1, 512, 640), (GU2, 640, 896)):
+                for job, lo, hi in ((GU1, 0, 256), (GU1, 256, 512), (GU2, 512, 768), (GU2, 768, 896)):
                     got = nn(rows, grad[256 * p : 256 * p + 256, lo:hi])
-                    col = lo if job == GU1 else 0
+                    col = lo if job == GU1 else lo - 512
                     for j in range(4):
                         store(
                             jobs[job].grad, (z, x + j // 2, j % 2), slice(row, row + 40), slice(col, col + hi - lo),
@@ -665,14 +668,15 @@
         def _(c):
             rows = r.turned[rows_at(0, c, 112), 256 * p : 256 * p + 256]
             for lo, hi in WIDE_TILES:
-                r.down[0:112, lo:hi] = nn(rows, r.cot[2 * p : 2 * p + 2, :, lo:hi].reshape(256, hi - lo))
+                r.down[:, lo:hi] = nn(rows, r.cot[2 * p : 2 * p + 2, :, lo:hi].reshape(256, hi - lo))
             z, x = lax.div(c, 2), 2 * lax.rem(c, 2)
             for j in range(4):
-                store(
-                    jobs[DN].grad, (z, x + j // 2, j % 2), slice(0, 32), slice(0, D), r.down[28 * j : 28 * j + 32], p
-                )
-
-    r.down[112:120] = jnp.zeros((8, D), F32)
+                r.lined[0:28] = r.down[28 * j : 28 * j + 28, 0:1152]
+                for m in range(7):
+                    r.lined[28:32, 128 * m : 128 * m + 128] = r.down[28 * j + 4 * m : 28 * j + 4 * m + 4, 1152:1280]
+                store(jobs[DN].grad, (z, x + j // 2, j % 2), slice(0, 32), slice(0, 1152), r.lined[...], p)
+
+    r.lined[...] = jnp.zeros((32, 1152), F32)
     swap1.take(0)
     feed(0)
     sum2.send_near(0)

time: 116 us -> 120 us (1.034)
  Pallas kernels: 114 us -> 118 us
    pallas_call x1, Pallas kernels: 111 us -> 114 us  [shards(): pl.pallas_call(layer_kernel, out_shape=(jax.ShapeDtypeStruct((FLAT, 128),...]
where the time goes in v8:
time: 120 us; the launch traced here: 118 us
  Pallas kernels  118 us (98%)
    pallas_call x1, Pallas kernels, shards(): pl.pallas_call(layer_kernel, out_shape=(jax.ShapeDtypeStruct((FLAT, 128),...  114 us
    pallas_call x1, Pallas kernels, adam(): pl.pallas_call(adam_kernel, out_shape=[jax.ShapeDtypeStruct((FLAT, 128),...  3.6 us

profile of v8, /device:TPU:0, one launch (start us, length us, event | category | flops | bytes accessed | tf_op | source)
XLA Modules:
  0.0 118.3 jit_solution(11789584404842038399)
XLA Ops:
  0.6 114.1 %shard_map.182 = (f32[1512,128]{1,0:T(8,128)}, bf16[128,1280]{1,0:T(8,128)(2,1)}, bf16[32,4096]{1,0:T(8,128)(2,1)}) custom-call(s32[1,128]{1,0:T(1,128)} %refs_0_.1, f32[1280]{0:T(1024)} %refs_1_.1, f32[1280]{0:T(1024)} %refs_2_.1, bf16[4,128,1280]{2,1,0:T(8,128)(2,1)} %bitcast.7, bf16[128,4096]{1,0:T(8,128)(2,1)} %refs_4_.1, bf16[4,128,1280]{2,1,0:T(8,128)(2,1)} %bitcast.8, ...), custom_call_target="tpu_custom_call" | custom-call | tf_op jit(solution)/shard_map/pallas_call | solution.py:881
  114.7 3.6 %shard_map.183 = (f32[1512,128]{1,0:T(8,128)}, f32[1512,128]{1,0:T(8,128)}, f32[1512,128]{1,0:T(8,128)}, bf16[128,1280]{1,0:T(8,128)(2,1)}, bf16[32,4096]{1,0:T(8,128)(2,1)}) custom-call(f32[1512,128]{1,0:T(8,128)} %get-tuple-element.13.summed, f32[1512,128]{1,0:T(8,128)} %bitcast.9, f32[1512,128]{1,0:T(8,128)} %bitcast.10, ...), custom_call_target="tpu_custom_call" | custom-call | tf_op jit(solution)/shard_map/pallas_call | solution.py:852
